TPU v7x, 128 devices: a whole 4x4x4 slice. The times are simulated.
128 devices in a mesh: bx: 16 (over z, y), by: 8 (over x, core).
Axes of the slice: x: 4, y: 4, z: 4, core: 2. Of those that a mesh axis runs over, the one named last changes fastest.
Arguments:
- vox_feats: bfloat16 [512, 8, 8, 512], P(('bx', 'by')), may hold values from -6 to 6
- block_coords: int32 [3, 512], P(None, ('bx', 'by')), may hold values from 0 to 95, as said below
- neighbors: int32 [27, 512], P(None, ('bx', 'by')), may hold values from -1 to 511, as said below
- conv_w: bfloat16 [3, 3, 3, 64, 64], replicated, may hold values from -0.15625 to 0.15625
- conv_b: float32 [64], replicated, may hold values from -3 to 3
- fold_w: bfloat16 [1024, 128], replicated, may hold values from -0.1875 to 0.1875
- fold_b: float32 [128], replicated, may hold values from -3 to 3
- map_w: bfloat16 [3, 3, 128, 128], replicated, may hold values from -0.1875 to 0.1875
- map_b: float32 [128], replicated, may hold values from -3 to 3
- cotangent: bfloat16 [768, 256, 128], P('bx', 'by'), may hold values from -6 to 6
Outputs:
- bev_map: bfloat16 [768, 256, 128], P('bx', 'by')
- feat_grad: float32 [512, 8, 8, 512], P(('bx', 'by'))
- conv_grads: float32 [3, 3, 3, 64, 64], replicated
- fold_grads: float32 [1024, 128], replicated
- map_grads: float32 [3, 3, 128, 128], replicated
Inputs may be any that keep to these rules, and one draw needn't show every extreme that they name: Row 0 of block_coords is a block's row of blocks (0 to 95), row 1 its column of blocks (0 to 31), row 2 its height block (0 or 1: height levels 8 h to 8 h + 7 of 16). The blocks at positions g * 32 to (g + 1) * 32 - 1 all lie in rows of blocks g * 6 to (g + 1) * 6 - 1. No two blocks share coordinates. `neighbors`: entry 9 (dx + 1) + 3 (dy + 1) + dz + 1 of a block's column is the position of the active block at block offset (dx, dy, dz), or -1 where there is none; entry 13 is the block itself. A neighbour of a block of positions g * 32 to (g + 1) * 32 - 1 lies at positions (g - 1) * 32 to (g + 2) * 32 - 1.
All inputs are finite; a program needn't handle non-finite values.
Results may differ from a plain program's by a relative error of at most 0.015.
Values may be sent and summed in bfloat16 or wider, within the bound.
A program may use at most 192 MiB of HBM per device.

v0:
```python
import functools

import jax
import jax.numpy as jnp
from jax import lax
from jax.experimental import pallas as pl
from jax.experimental.pallas import tpu as pltpu
from jax.sharding import PartitionSpec as P

MESH = pl.DeviceIdType.MESH
BF = jnp.bfloat16
F32 = jnp.float32
BS = 8
TR = 6
TC = 4
NB = 4
NX = 16
NY = 8
GROUP = NB * NY
ROWS = TR * BS
COLS = TC * BS
VMEM = pl.BlockSpec(memory_space=pltpu.VMEM)
SMEM = pl.BlockSpec(memory_space=pltpu.SMEM)
DMA = pltpu.SemaphoreType.DMA
CAT = 3072
CHUNK = CAT // NY
SLICE = CHUNK // NX


def place():
    return lax.axis_index("bx"), lax.axis_index("by")


def remote(src, dst, send, recv, device):
    return pltpu.make_async_remote_copy(
        src_ref=src,
        dst_ref=dst,
        send_sem=send,
        recv_sem=recv,
        device_id=device,
        device_id_type=MESH,
    )


def signal(device):
    pl.semaphore_signal(
        pltpu.get_barrier_semaphore(), inc=1, device_id=device, device_id_type=MESH
    )


def slope(pre):
    s = jax.nn.sigmoid(pre)
    return s * (1.0 + pre * (1.0 - s))


def rounded(v):
    return v.astype(BF).astype(F32)


def group_barrier():
    bx, by = place()
    core = by % 2
    for k in range(1, NY):
        signal((bx, (by + k) % NY))
    prev = bx > 0
    after = bx < NX - 1

    @pl.when(prev)
    def _():
        for j in range(NY // 2):
            signal((bx - 1, core + 2 * j))

    @pl.when(after)
    def _():
        for j in range(NY // 2):
            signal((bx + 1, core + 2 * j))

    count = NY - 1 + 4 * prev.astype(jnp.int32) + 4 * after.astype(jnp.int32)
    pl.semaphore_wait(pltpu.get_barrier_semaphore(), count)


def pack_faces(cur, msg, coords):
    lane = lax.broadcasted_iota(jnp.int32, (32, 128), 1)

    def flat(v):
        return jnp.concatenate([v[:, t * 128 : (t + 1) * 128] for t in range(4)], 0)

    def one(n, carry):
        high = coords[2, n].astype(F32)
        msg[n, 0] = flat(cur[0, n]).astype(BF)
        msg[n, 1] = flat(cur[7, n]).astype(BF)
        msg[n, 2] = flat(cur[:, n, 0, :]).astype(BF)
        msg[n, 3] = flat(cur[:, n, 7, :]).astype(BF)
        top = cur[:, n, :, 384:512].reshape(64, 128)
        low = cur[:, n, :, 0:128].reshape(64, 128)
        face = pltpu.roll(top, 64, 1) * (1.0 - high) + low * high
        msg[n, 4] = jnp.where(lane < 64, face[0:32], pltpu.roll(face[32:64], 64, 1)).astype(BF)
        return carry

    lax.fori_loop(0, NB, one, 0)


class Faces:
    def __init__(self, msg, pool, side, own_s, fwd_s, side_s, sfwd_s, own_r, side_r):
        self.msg, self.pool, self.side = msg, pool, side
        self.own_s, self.fwd_s, self.side_s, self.sfwd_s = own_s, fwd_s, side_s, sfwd_s
        self.own_r, self.side_r = own_r, side_r
        self.bx, self.by = place()
        self.core = self.by % 2
        self.mate = self.by + 1 - 2 * self.core

    def first(self):
        bx, by = self.bx, self.by
        mine = pl.ds(by * NB, NB)
        out = [
            remote(self.msg, self.pool.at[mine], self.own_s.at[k], self.own_r.at[by], (bx, peer))
            for k, peer in enumerate([self.mate] + [(by + 2 * k) % NY for k in (1, 2, 3)])
        ]
        return out

    def sides(self, to):
        bx, by = self.bx, self.by
        mine = pl.ds(by * NB, NB)
        part, step = ((1, 1), (0, -1))[to]
        return [
            remote(
                self.msg.at[:, part],
                self.side.at[to, mine],
                self.side_s.at[to, j],
                self.side_r.at[to, by],
                (bx + step, self.core + 2 * j),
            )
            for j in range(4)
        ]

    def has(self, to):
        return (self.bx > 0, self.bx < NX - 1)[to]

    def sends(self, to):
        return self.has(1 - to)

    def start(self):
        for c in self.first():
            c.start()
        for to in range(2):

            @pl.when(self.sends(to))
            def _(to=to):
                for c in self.sides(to):
                    c.start()

        self.pool[pl.ds(self.by * NB, NB)] = self.msg[...]

    def own_landed(self, src, k):
        at = self.pool.at[pl.ds(src * NB, NB)]
        return remote(at, at, self.fwd_s.at[k], self.own_r.at[src], (self.bx, self.mate))

    def side_landed(self, to, src, j):
        at = self.side.at[to, pl.ds(src * NB, NB)]
        return remote(at, at, self.sfwd_s.at[to, j], self.side_r.at[to, src], (self.bx, self.mate))

    def forward(self):
        for k in (1, 3, 2):
            c = self.own_landed((self.by + 2 * k) % NY, k - 1)
            c.wait_recv()
            c.start()
        for to in range(2):

            @pl.when(self.has(to))
            def _(to=to):
                for j in range(4):
                    c = self.side_landed(to, self.core + 2 * j, j)
                    c.wait_recv()
                    c.start()

    def finish(self):
        for k in range(4):
            self.own_landed((self.mate + 2 * k) % NY, 0).wait_recv()
        for to in range(2):

            @pl.when(self.has(to))
            def _(to=to):
                for j in range(4):
                    self.side_landed(to, 1 - self.core + 2 * j, j).wait_recv()

    def drain(self):
        for c in self.first():
            c.wait_send()
        for k in (1, 2, 3):
            self.own_landed((self.by + 2 * k) % NY, k - 1).wait_send()
        for to in range(2):

            @pl.when(self.sends(to))
            def _(to=to):
                for c in self.sides(to):
                    c.wait_send()

            @pl.when(self.has(to))
            def _(to=to):
                for j in range(4):
                    self.side_landed(to, self.core + 2 * j, j).wait_send()


FACE_SCRATCH = [
    pltpu.VMEM((NB, 5, 32, 128), BF),
    pltpu.VMEM((GROUP + 1, 5, 32, 128), BF),
    pltpu.VMEM((2, GROUP + 1, 32, 128), BF),
    DMA((4,)),
    DMA((3,)),
    DMA((2, 4)),
    DMA((2, 4)),
    DMA((NY,)),
    DMA((2, NY)),
]


def assemble(cur, pool, side, own_at, side_at, shifted, edge):
    low = lax.broadcasted_iota(jnp.int32, (8, 128), 1) < 64
    sub = lax.broadcasted_iota(jnp.int32, (8, 128), 0)

    def one(n, carry):
        def face(part, k):
            return pool[own_at[k, n], part].astype(F32)

        def xface(dx, k):
            near = face(1 if dx < 0 else 0, k)
            return near + side[0 if dx < 0 else 1, side_at[k, n]].astype(F32)

        def tiles(v):
            return [v[t * 8 : (t + 1) * 8] for t in range(4)]

        def turn(v):
            return pltpu.roll(v, 64, 1)

        def padz(core, before, after):
            r = [turn(t) for t in core]
            return (
                [jnp.where(low, before, r[0])]
                + [jnp.where(low, r[t - 1], r[t]) for t in (1, 2, 3)]
                + [jnp.where(low, r[3], after)]
            )

        def put(x, t, mid, above, below):
            row = pl.multiple_of((x * NB + n) * 8, 8)
            at = (pl.ds(row, 8), pl.ds(t * 128, 128))
            shifted[(1, *at)] = mid
            shifted[(0, *at)] = jnp.where(sub == 0, above, pltpu.roll(mid, 1, 0))
            shifted[(2, *at)] = jnp.where(sub == 7, below, pltpu.roll(mid, 7, 0))

        for x, dx in ((0, -1), (9, 1)):
            z = []
            for dy in range(3):
                k = 9 * (dx + 1) + 3 * dy
                z.append(
                    padz(tiles(xface(dx, k + 1)), turn(xface(dx, k)[24:32]), turn(xface(dx, k + 2)[0:8]))
                )
            for t in range(5):
                put(x, t, z[1][t], pltpu.roll(z[0][t], 1, 0), pltpu.roll(z[2][t], 7, 0))
        for i, (k, part) in enumerate(((9, 3), (15, 2))):
            z = padz(tiles(face(part, k + 1)), turn(face(part, k)[24:32]), turn(face(part, k + 2)[0:8]))
            for t in range(5):
                edge[i, :, t * 128 : (t + 1) * 128] = z[t]
        under = face(4, 12)
        over = face(4, 14)
        for x in range(BS):
            at = slice(x % 4 * 8, x % 4 * 8 + 8)
            before = under[at] if x < 4 else turn(under[at])
            after = turn(over[at]) if x < 4 else over[at]
            z = padz([cur[x, n, :, t * 128 : (t + 1) * 128] for t in range(4)], before, after)
            for t in range(5):
                lanes = slice(t * 128, (t + 1) * 128)
                put(x + 1, t, z[t], edge[0, x : x + 1, lanes], edge[1, x : x + 1, lanes])
        return carry

    lax.fori_loop(0, NB, one, 0)


def owner_forward(
    vox, conv_w, conv_b, fold_w, coord_tile, coords, own_at, side_at,
    pre_out, act_out, wide_out, part_out, coords_out,
    cur, shifted, edge, toep, fold_both, part,
    msg, pool, side, own_s, fwd_s, side_s, sfwd_s, own_r, side_r,
    part_s, part_r, coord_s, coord_r,
):
    bx, by = place()
    faces = Faces(msg, pool, side, own_s, fwd_s, side_s, sfwd_s, own_r, side_r)
    for n in range(NB):
        cur[:, n] = vox[n].astype(F32)
    pack_faces(cur, msg, coords)
    group_barrier()
    faces.start()
    tell = [
        remote(coord_tile, coords_out.at[by], coord_s.at[k], coord_r.at[by], (bx, (by + k) % NY))
        for k in range(1, NY)
    ]
    for c in tell:
        c.start()
    coords_out[by] = coord_tile[...]
    pool[GROUP] = jnp.zeros((5, 32, 128), BF)
    for to in range(2):
        side[to, GROUP] = jnp.zeros((32, 128), BF)
    blank = jnp.zeros((64, 64), F32)

    def build(tap, carry):
        w = [blank] + [conv_w[tap * 3 + k].astype(F32) for k in range(3)] + [blank]
        for z in range(4):
            toep[tap, z * 64 : (z + 1) * 64, :] = jnp.concatenate([w[z + 1], w[z]], 1).astype(BF)
        return carry

    lax.fori_loop(0, 9, build, 0)
    faces.forward()
    faces.finish()
    assemble(cur, pool, side, own_at, side_at, shifted, edge)
    for e in range(3):
        wide_out[:, e * 640 : (e + 1) * 640] = shifted[e].astype(BF)
    bias = conv_b[...]
    for group in range(4):
        total = bias
        for a in range(3):
            for e in range(3):
                lhs = wide_out[a * 32 : a * 32 + 256, e * 640 + group * 128 : e * 640 + group * 128 + 256]
                total = total + jnp.dot(lhs, toep[a * 3 + e], preferred_element_type=F32)
        lanes = slice(group * 128, (group + 1) * 128)
        pre_out[:, lanes] = total
        act_out[:, lanes] = (total * jax.nn.sigmoid(total)).astype(BF)
    both = jnp.concatenate(
        [
            jnp.dot(act_out[...], fold_w[h], preferred_element_type=F32) for h in range(2)
        ],
        1,
    )
    fold_both[...] = both.reshape(BS, NB, BS, 256)
    for n in range(NB):
        high = coords[2, n].astype(F32)
        one = fold_both[:, n, :, 0:128] * (1.0 - high) + fold_both[:, n, :, 128:256] * high
        part[n] = one.reshape(64, 128).astype(BF)
    mine = pl.ds(by * NB, NB)
    give = [
        remote(part, part_out.at[mine], part_s.at[k], part_r.at[by], (bx, (by + k) % NY))
        for k in range(1, NY)
    ]
    for c in give:
        c.start()
    part_out[mine] = part[...]
    for k in range(1, NY):
        src = (by + k) % NY
        remote(part, part_out.at[pl.ds(src * NB, NB)], part_s.at[k], part_r.at[src], (bx, src)).wait_recv()
        remote(coord_tile, coords_out.at[src], coord_s.at[k], coord_r.at[src], (bx, src)).wait_recv()
    for c in give + tell:
        c.wait_send()
    faces.drain()


NEAR = [(-1, 0), (1, 0), (0, -1), (0, 1), (-1, -1), (-1, 1), (1, -1), (1, 1)]


class Rim:
    def __init__(self, row_out, col_out, row_in, col_in, corner_in, send, recv):
        self.row_out, self.col_out = row_out, col_out
        self.row_in, self.col_in, self.corner_in = row_in, col_in, corner_in
        self.send, self.recv = send, recv
        self.bx, self.by = place()

    def exists(self, d):
        dx, dy = NEAR[d]
        ok = None
        for v, step, size in ((self.bx, dx, NX), (self.by, dy, NY)):
            if step:
                here = v > 0 if step < 0 else v < size - 1
                ok = here if ok is None else ok & here
        return ok

    def copy(self, d):
        dx, dy = NEAR[d]
        back = NEAR.index((-dx, -dy))
        if dy == 0:
            src, dst = self.row_out.at[d], self.row_in.at[back]
        elif dx == 0:
            src, dst = self.col_out.at[d - 2], self.col_in.at[back - 2]
        else:
            src = self.row_out.at[0 if dx < 0 else 1, pl.ds(0 if dy < 0 else 16, 16)]
            dst = self.corner_in.at[back - 4]
        return remote(src, dst, self.send.at[d], self.recv.at[back], (self.bx + dx, self.by + dy))

    def landing(self, d):
        dx, dy = NEAR[d]
        if dy == 0:
            return self.row_in.at[d]
        if dx == 0:
            return self.col_in.at[d - 2]
        return self.corner_in.at[d - 4]

    def start(self, plane):
        self.row_out[0] = plane[0].astype(BF)
        self.row_out[1] = plane[ROWS - 1].astype(BF)
        self.col_out[0] = plane[:, 0, :].astype(BF)
        self.col_out[1] = plane[:, COLS - 1, :].astype(BF)
        for d in range(8):

            @pl.when(self.exists(d))
            def _(d=d):
                self.copy(d).start()

            @pl.when(jnp.logical_not(self.exists(d)))
            def _(d=d):
                at = self.landing(d)
                at[...] = jnp.zeros(at.shape, BF)

    def finish(self):
        for d in range(8):

            @pl.when(self.exists(d))
            def _(d=d):
                dx, dy = NEAR[d]
                at = self.landing(d)
                remote(at, at, self.send.at[d], self.recv.at[d], (self.bx + dx, self.by + dy)).wait_recv()

    def drain(self):
        for d in range(8):

            @pl.when(self.exists(d))
            def _(d=d):
                self.copy(d).wait_send()


def spread(plane, rim, side32, out):
    side32[0] = rim.col_in[0].astype(F32)
    side32[1] = rim.col_in[1].astype(F32)
    j = lax.broadcasted_iota(jnp.int32, (COLS, 128), 0)

    def put(at, row, left, right):
        rows = pl.ds(pl.multiple_of(at * COLS, COLS), COLS)
        out[rows, 0:128] = jnp.where(j == 0, left, pltpu.roll(row, 1, 0)).astype(BF)
        out[rows, 128:256] = row.astype(BF)
        out[rows, 256:384] = jnp.where(j == COLS - 1, right, pltpu.roll(row, COLS - 1, 0)).astype(BF)

    def inner(i, carry):
        put(i + 1, plane[i], side32[0, pl.ds(i, 1), :], side32[1, pl.ds(i, 1), :])
        return carry

    lax.fori_loop(0, ROWS, inner, 0)
    corner = [rim.corner_in[c].astype(F32) for c in range(4)]
    put(0, rim.row_in[0].astype(F32), corner[0][15:16], corner[1][0:1])
    put(ROWS + 1, rim.row_in[1].astype(F32), corner[2][15:16], corner[3][0:1])


def map_kernel(
    part, table, block_slot, cot, map_w, map_b, fold_b,
    bev_out, grads_out, back_out,
    fold, plane, gplane, spread_mid, spread_grad, flat_grad, side32, slots, ready,
    row_out, col_out, row_in, col_in, corner_in, send, recv,
    back_s, back_r,
):
    bx, by = place()
    rims = [
        Rim(row_out.at[p], col_out.at[p], row_in.at[p], col_in.at[p], corner_in.at[p], send.at[p], recv.at[p])
        for p in range(2)
    ]
    for k in range(1, NY):
        signal((bx, (by + k) % NY))
    count = jnp.int32(NY - 1)
    for d, (dx, dy) in enumerate(NEAR):
        if dx:

            @pl.when(rims[0].exists(d))
            def _(dx=dx, dy=dy):
                signal((bx + dx, by + dy))

            count = count + rims[0].exists(d).astype(jnp.int32)
    for r in range(TR):
        for c in range(TC):
            total = fold_b[...]
            for h in range(2):
                at = table[(r * TC + c) * 2 + h]
                here = (at < GROUP).astype(F32)
                total = total + part[jnp.minimum(at, GROUP - 1)].astype(F32) * here
            total = jnp.broadcast_to(total, (64, 128))
            where = (slice(r * BS, (r + 1) * BS), slice(c * BS, (c + 1) * BS))
            fold[where] = total.reshape(BS, BS, 128)
            plane[where] = rounded(total * jax.nn.sigmoid(total)).reshape(BS, BS, 128)
    pl.semaphore_wait(pltpu.get_barrier_semaphore(), count)
    rims[0].start(plane)
    rims[0].finish()
    spread(plane, rims[0], side32, spread_mid)

    def ahead(i, carry):
        start = pl.multiple_of(i * 256, 256)
        total = map_b[...]
        for a in range(3):
            lhs = spread_mid[pl.ds(start + a * COLS, 256), :]
            total = total + jnp.dot(lhs, map_w[a], preferred_element_type=F32)
        bev_out[pl.ds(i * BS, BS)] = (total * jax.nn.sigmoid(total)).reshape(BS, COLS, 128).astype(BF)
        g = cot[pl.ds(i * BS, BS)].astype(F32).reshape(256, 128) * slope(total)
        flat_grad[pl.ds(start, 256), :] = g.astype(BF)
        gplane[pl.ds(i * BS, BS)] = rounded(g).reshape(BS, COLS, 128)
        return carry

    lax.fori_loop(0, TR, ahead, 0)
    rims[1].start(gplane)
    turned = gplane[...].reshape(ROWS * COLS, 128).T.astype(BF)
    for a in range(3):
        got = jnp.dot(turned, spread_mid[a * COLS : a * COLS + ROWS * COLS, :], preferred_element_type=F32)
        for e in range(3):
            grads_out[a * 3 + e] = got[:, e * 128 : (e + 1) * 128].T
    rims[1].finish()
    spread(gplane, rims[1], side32, spread_grad)

    def behind(i, carry):
        start = pl.multiple_of(i * 256, 256)
        total = None
        for a in range(3):
            for e in range(3):
                lhs = spread_grad[pl.ds(start + a * COLS, 256), e * 128 : (e + 1) * 128]
                w = map_w[2 - a, (2 - e) * 128 : (3 - e) * 128, :]
                one = lax.dot_general(lhs, w, (((1,), (1,)), ((), ())), preferred_element_type=F32)
                total = one if total is None else total + one
        pre = fold[pl.ds(i * BS, BS)].reshape(256, 128)
        back = (total * slope(pre)).reshape(BS, COLS, 128)
        for c in range(TC):
            slots[i * TC + c] = back[:, c * BS : (c + 1) * BS, :].reshape(64, 128).astype(BF)
        return carry

    lax.fori_loop(0, TR, behind, 0)

    def fill(b, carry):
        ready[b] = slots[block_slot[b]]
        return carry

    lax.fori_loop(0, GROUP, fill, 0)
    give = []
    for k in range(1, NY):
        peer = (by + k) % NY
        give.append(
            remote(ready.at[pl.ds(peer * NB, NB)], back_out.at[by], back_s.at[k], back_r.at[by], (bx, peer))
        )
    for c in give:
        c.start()
    back_out[by] = ready[pl.ds(by * NB, NB)]
    for k in range(1, NY):
        src = (by + k) % NY
        remote(ready.at[pl.ds(0, NB)], back_out.at[src], back_s.at[k], back_r.at[src], (bx, src)).wait_recv()
    for c in give:
        c.wait_send()
    for rim in rims:
        rim.drain()


def owner_backward(
    pre, act, wide, back, conv_w, fold_w, coords, own_at, side_at,
    feat_out, conv_out, fold_out,
    cur, shifted, edge, toep, wide2, split, cur_bf,
    msg, pool, side, own_s, fwd_s, side_s, sfwd_s, own_r, side_r,
):
    faces = Faces(msg, pool, side, own_s, fwd_s, side_s, sfwd_s, own_r, side_r)
    for n in range(NB):
        high = coords[2, n].astype(F32)
        mine = back[coords[1, n] // TC, n].astype(F32).reshape(BS, BS, 128)
        split[:, n, :, 0:128] = mine * (1.0 - high)
        split[:, n, :, 128:256] = mine * high
    both = split[...].reshape(256, 256)
    act_grad = None
    for h in range(2):
        one = lax.dot_general(
            both[:, h * 128 : (h + 1) * 128].astype(BF), fold_w[h], (((1,), (1,)), ((), ())), preferred_element_type=F32
        )
        act_grad = one if act_grad is None else act_grad + one
    grad = rounded(rounded(act_grad) * slope(pre[...]))
    cur[...] = grad.reshape(BS, NB, BS, 512)
    cur_bf[...] = grad.astype(BF)
    pack_faces(cur, msg, coords)
    group_barrier()
    faces.start()
    pool[GROUP] = jnp.zeros((5, 32, 128), BF)
    for to in range(2):
        side[to, GROUP] = jnp.zeros((32, 128), BF)
    turned_fold = both.T.astype(BF)
    got = jnp.dot(turned_fold, act[...], preferred_element_type=F32)
    for h in range(2):
        fold_out[h] = got[h * 128 : (h + 1) * 128].T
    blank = jnp.zeros((64, 64), F32)

    def build(tap, carry):
        w = [conv_w[tap * 3 + k].astype(F32) for k in range(3)]
        rows = ((w[2], w[1], w[0], blank), (blank, w[2], w[1], w[0]))
        for z in range(2):
            for half in range(2):
                pair = jnp.concatenate(rows[z][half * 2 : half * 2 + 2], 1)
                toep[tap, z * 64 : (z + 1) * 64, half * 128 : (half + 1) * 128] = pair.astype(BF)
        return carry

    lax.fori_loop(0, 9, build, 0)
    faces.forward()
    turned = [cur_bf[:, g * 128 : (g + 1) * 128].astype(F32).T.astype(BF) for g in range(4)]
    low = lax.broadcasted_iota(jnp.int32, (96, 128), 1) < 64
    for a in range(3):
        for e in range(3):
            total = None
            for g in range(4):
                rhs = wide[a * 32 : a * 32 + 256, e * 640 + g * 128 : e * 640 + g * 128 + 256]
                one = jnp.dot(turned[g], rhs, preferred_element_type=F32)
                total = one if total is None else total + one
            total = total.T
            summed = total[0:192] + pltpu.roll(total[64:256], 64, 1)
            conv_out[a * 3 + e] = jnp.where(low, summed[0:96], pltpu.roll(summed[96:192], 64, 1))
    faces.finish()
    assemble(cur, pool, side, own_at, side_at, shifted, edge)
    for e in range(3):
        wide2[:, e * 640 : (e + 1) * 640] = shifted[e].astype(BF)
    for g in range(4):
        total = None
        for a in range(3):
            for e in range(3):
                lhs = wide2[a * 32 : a * 32 + 256, e * 640 + g * 128 : e * 640 + g * 128 + 256]
                one = lax.dot_general(
                    lhs, toep[(2 - a) * 3 + 2 - e], (((1,), (1,)), ((), ())), preferred_element_type=F32
                )
                total = one if total is None else total + one
        view = total.reshape(BS, NB, BS, 128)
        for n in range(NB):
            feat_out[n, :, :, g * 128 : (g + 1) * 128] = view[:, n]
    faces.drain()


def reduce_kernel(
    map_part, fold_part, conv_part,
    map_out, fold_out, conv_out,
    cat, first, acc, second, summed, third, chunk, fourth,
    s1, r1, s2, r2, s3, r3, s4, r4,
):
    bx, by = place()
    for k in range(1, NY):
        signal((bx, (by + k) % NY))
    for k in range(1, NX):
        signal(((bx + k) % NX, by))
    for t in range(9):
        cat[t * 128 : (t + 1) * 128] = map_part[t].astype(BF)
    for h in range(2):
        cat[1152 + h * 512 : 1152 + (h + 1) * 512] = fold_part[h].astype(BF)
    for t in range(9):
        cat[2176 + t * 96 : 2176 + (t + 1) * 96] = conv_part[t].astype(BF)
    cat[3040:3072] = jnp.zeros((32, 128), BF)
    pl.semaphore_wait(pltpu.get_barrier_semaphore(), NY + NX - 2)

    def piece(i):
        return pl.ds(pl.multiple_of(i * CHUNK, CHUNK), CHUNK)

    def small(i):
        return pl.ds(pl.multiple_of(i * SLICE, SLICE), SLICE)

    def peers_y(make):
        return [make(k, (by + k) % NY) for k in range(1, NY)]

    def peers_x(make):
        return [make(k, (bx + k) % NX) for k in range(1, NX)]

    out1 = peers_y(lambda k, p: remote(cat.at[piece(p)], first.at[by], s1.at[k], r1.at[by], (bx, p)))
    for c in out1:
        c.start()
    acc[...] = cat[piece(by)].astype(F32)
    for c in peers_y(lambda k, p: remote(cat.at[piece(p)], first.at[p], s1.at[k], r1.at[p], (bx, p))):
        c.wait_recv()
    for k in range(1, NY):
        acc[...] += first[(by + k) % NY].astype(F32)
    out2 = peers_x(lambda k, p: remote(acc.at[small(p)], second.at[bx], s2.at[k], r2.at[bx], (p, by)))
    for c in out2:
        c.start()
    total = acc[small(bx)]
    for c in peers_x(lambda k, p: remote(acc.at[small(p)], second.at[p], s2.at[k], r2.at[p], (p, by))):
        c.wait_recv()
    for k in range(1, NX):
        total = total + second[(bx + k) % NX]
    summed[...] = total
    out3 = peers_x(lambda k, p: remote(summed, third.at[small(bx)], s3.at[k], r3.at[bx], (p, by)))
    for c in out3:
        c.start()
    third[small(bx)] = total
    for c in peers_x(lambda k, p: remote(summed, third.at[small(p)], s3.at[k], r3.at[p], (p, by))):
        c.wait_recv()
    chunk[...] = third[...].astype(BF)
    out4 = peers_y(lambda k, p: remote(chunk, fourth.at[piece(by)], s4.at[k], r4.at[by], (bx, p)))
    for c in out4:
        c.start()
    fourth[piece(by)] = chunk[...]
    for c in peers_y(lambda k, p: remote(chunk, fourth.at[piece(p)], s4.at[k], r4.at[p], (bx, p))):
        c.wait_recv()
    for t in range(9):
        map_out[t] = fourth[t * 128 : (t + 1) * 128].astype(F32)
    for h in range(2):
        fold_out[h] = fourth[1152 + h * 512 : 1152 + (h + 1) * 512].astype(F32)
    for t in range(9):
        v = fourth[2176 + t * 96 : 2176 + (t + 1) * 96].astype(F32)
        conv_out[t, 0:96] = v[:, 0:64]
        conv_out[t, 96:192] = v[:, 64:128]
    for c in out1 + out2 + out3 + out4:
        c.wait_send()


def call(kernel, ident, ins, outs, scratch):
    return pl.pallas_call(
        kernel,
        in_specs=ins,
        out_specs=[VMEM] * len(outs),
        out_shape=[jax.ShapeDtypeStruct(s, t) for s, t in outs],
        scratch_shapes=scratch,
        compiler_params=pltpu.CompilerParams(
            collective_id=ident, has_side_effects=True, vmem_limit_bytes=50 * 2**20
        ),
    )


def body(vox_feats, block_coords, neighbors, conv_w, conv_b, fold_w, fold_b, map_w, map_b, cotangent):
    bx, by = place()
    taps = conv_w.reshape(27, 64, 64)
    fold_w2 = fold_w.reshape(2, 512, 128)
    inside = neighbors - bx * GROUP
    own_at = jnp.where((neighbors >= 0) & (inside >= 0) & (inside < GROUP), inside, GROUP)
    step = (jnp.arange(27) // 9 - 1)[:, None]
    beside = neighbors - (bx + step) * GROUP
    side_at = jnp.where(
        (neighbors >= 0) & (step != 0) & (beside >= 0) & (beside < GROUP), beside, GROUP
    )
    coord_tile = jnp.pad(block_coords, ((0, 5), (0, 124)))
    pre, act, wide, part, coords_all = call(
        owner_forward,
        1,
        [VMEM] * 5 + [SMEM] * 3,
        [
            ((256, 512), F32),
            ((256, 512), BF),
            ((320, 1920), BF),
            ((GROUP, 64, 128), BF),
            ((NY, 8, 128), jnp.int32),
        ],
        [
            pltpu.VMEM((BS, NB, BS, 512), F32),
            pltpu.VMEM((3, 320, 640), F32),
            pltpu.VMEM((2, 8, 640), F32),
            pltpu.VMEM((9, 256, 128), BF),
            pltpu.VMEM((BS, NB, BS, 256), F32),
            pltpu.VMEM((NB, 64, 128), BF),
            *FACE_SCRATCH,
            DMA((NY,)),
            DMA((NY,)),
            DMA((NY,)),
            DMA((NY,)),
        ],
    )(
        vox_feats,
        taps,
        jnp.tile(conv_b, 2)[None],
        fold_w2,
        coord_tile,
        block_coords,
        own_at,
        side_at,
    )
    group = coords_all[:, :3, :NB].transpose(1, 0, 2).reshape(3, GROUP)
    row, col = group[0] - bx * TR, group[1] - by * TC
    within = (col >= 0) & (col < TC)
    slot = row * TC + col
    key = jnp.where(within, slot * 2 + group[2], -1)
    match = key[None, :] == jnp.arange(TR * TC * 2)[:, None]
    table = jnp.min(jnp.where(match, jnp.arange(GROUP)[None, :], GROUP), 1).astype(jnp.int32)
    block_slot = jnp.clip(jnp.where(within, slot, 0), 0, TR * TC - 1).astype(jnp.int32)
    rim_scratch = [
        pltpu.VMEM((2, 2, COLS, 128), BF),
        pltpu.VMEM((2, 2, ROWS, 128), BF),
        pltpu.VMEM((2, 2, COLS, 128), BF),
        pltpu.VMEM((2, 2, ROWS, 128), BF),
        pltpu.VMEM((2, 4, 16, 128), BF),
        DMA((2, 8)),
        DMA((2, 8)),
    ]
    bev_map, map_part, back = call(
        map_kernel,
        2,
        [VMEM, SMEM, SMEM, VMEM, VMEM, VMEM, VMEM],
        [
            ((ROWS, COLS, 128), BF),
            ((9, 128, 128), F32),
            ((NY, NB, 64, 128), BF),
        ],
        [
            pltpu.VMEM((ROWS, COLS, 128), F32),
            pltpu.VMEM((ROWS, COLS, 128), F32),
            pltpu.VMEM((ROWS, COLS, 128), F32),
            pltpu.VMEM(((ROWS + 2) * COLS, 384), BF),
            pltpu.VMEM(((ROWS + 2) * COLS, 384), BF),
            pltpu.VMEM((ROWS * COLS, 128), BF),
            pltpu.VMEM((2, ROWS, 128), F32),
            pltpu.VMEM((TR * TC, 64, 128), BF),
            pltpu.VMEM((GROUP, 64, 128), BF),
            *rim_scratch,
            DMA((NY,)),
            DMA((NY,)),
        ],
    )(part, table, block_slot, cotangent, map_w.reshape(3, 384, 128), map_b[None], fold_b[None])
    feat_grad, conv_part, fold_part = call(
        owner_backward,
        3,
        [VMEM] * 6 + [SMEM] * 3,
        [
            ((NB, BS, BS, 512), F32),
            ((9, 96, 128), F32),
            ((2, 512, 128), F32),
        ],
        [
            pltpu.VMEM((BS, NB, BS, 512), F32),
            pltpu.VMEM((3, 320, 640), F32),
            pltpu.VMEM((2, 8, 640), F32),
            pltpu.VMEM((9, 128, 256), BF),
            pltpu.VMEM((320, 1920), BF),
            pltpu.VMEM((BS, NB, BS, 256), F32),
            pltpu.VMEM((256, 512), BF),
            *FACE_SCRATCH,
        ],
    )(pre, act, wide, back, taps, fold_w2, block_coords, own_at, side_at)
    map_grads, fold_grads, conv_grads = call(
        reduce_kernel,
        4,
        [VMEM] * 3,
        [
            ((9, 128, 128), F32),
            ((2, 512, 128), F32),
            ((9, 192, 64), F32),
        ],
        [
            pltpu.VMEM((CAT, 128), BF),
            pltpu.VMEM((NY, CHUNK, 128), BF),
            pltpu.VMEM((CHUNK, 128), F32),
            pltpu.VMEM((NX, SLICE, 128), F32),
            pltpu.VMEM((SLICE, 128), F32),
            pltpu.VMEM((CHUNK, 128), F32),
            pltpu.VMEM((CHUNK, 128), BF),
            pltpu.VMEM((CAT, 128), BF),
            *[DMA((size,)) for size in (NY, NY, NX, NX, NX, NX, NY, NY)],
        ],
    )(map_part, fold_part, conv_part)
    return (
        bev_map,
        feat_grad,
        conv_grads.reshape(3, 3, 3, 64, 64),
        fold_grads.reshape(1024, 128),
        map_grads.reshape(3, 3, 128, 128),
    )


def solution(mesh):
    placed = (
        P(("bx", "by"), None, None, None),
        P(None, ("bx", "by")),
        P(None, ("bx", "by")),
        P(),
        P(),
        P(),
        P(),
        P(),
        P(),
        P("bx", "by", None),
    )
    return jax.shard_map(
        body,
        mesh=mesh,
        in_specs=placed,
        out_specs=(P("bx", "by", None), P(("bx", "by"), None, None, None), P(), P(), P()),
        check_vma=False,
    )
```

profile of v0, /device:TPU:1, one launch (start us, length us, event | category | flops | bytes accessed | tf_op | source)
XLA Modules:
  0.0 132.9 jit_solution(7328054233969975917)
XLA Ops:
  0.7 0.7 tile.2
  1.3 0.1 broadcast_in_dim_tile.3.conv_b
  1.4 0.7 pad.4.coord_tile
  2.1 0.8 copy.24
  2.9 0.1 and_select_fusion
  3.0 1.0 copy-done
  4.0 0.9 copy-done.3
  4.9 0.9 copy-done.7
  5.9 0.7 copy-done.8
  6.6 31.8 %shard_map.137 = (f32[256,512]{1,0:T(8,128)S(1)}, bf16[256,512]{1,0:T(8,128)(2,1)S(1)}, bf16[320,1920]{1,0:T(8,128)(2,1)S(1)}, bf16[32,64,128]{2,1,0:T(8,128)(2,1)S(1)}, s32[8,8,128]{2,1,0:T(8,128)S(1)}) custom-call(bf16[4,8,8,512]{3,2,1,0:T(8,128)(2,1)S(1)} %copy-done.7, bf16[27,64,64]{2,1,0:T(8,128)(2,1)S(1)} %bitcast.10, ...), custom_call_target="tpu_custom_call" | custom-call | tf_op jit(solution)/shard_map/pallas_call | solution.py:723
  38.4 1.0 copy-done.2
  39.5 0.1 and.53
  39.8 0.1 select_reduce_fusion.table
  39.9 1.0 copy-done.6
  40.9 0.7 copy-done.10
  41.5 0.7 copy-done.11
  42.2 23.3 %shard_map.138 = (bf16[48,32,128]{2,1,0:T(8,128)(2,1)S(1)}, f32[9,128,128]{2,1,0:T(8,128)S(1)}, bf16[8,4,64,128]{3,2,1,0:T(8,128)(2,1)S(1)}) custom-call(bf16[32,64,128]{2,1,0:T(8,128)(2,1)S(1)} %get-tuple-element.19.part, s32[48]{0:T(128)S(1)} %select_reduce_fusion.table, s32[32]{0:T(128)S(1)} %get-tuple-element.37.block_slot, ...), custom_call_target="tpu_custom_call" | custom-call | tf_op jit(solution)/shard_map/pallas_call | solution.py:774
  65.5 22.9 %shard_map.139 = (f32[4,8,8,512]{3,2,1,0:T(8,128)S(1)}, f32[9,96,128]{2,1,0:T(8,128)S(1)}, f32[2,512,128]{2,1,0:T(8,128)S(1)}) custom-call(f32[256,512]{1,0:T(8,128)S(1)} %get-tuple-element.22.pre, bf16[256,512]{1,0:T(8,128)(2,1)S(1)} %get-tuple-element.23.act, bf16[320,1920]{1,0:T(8,128)(2,1)} %copy-done.2, ...), custom_call_target="tpu_custom_call" | custom-call | tf_op jit(solution)/shard_map/pallas_call | solution.py:798
  88.4 40.5 %shard_map.140 = (f32[9,128,128]{2,1,0:T(8,128)S(1)}, f32[2,512,128]{2,1,0:T(8,128)S(1)}, f32[9,192,64]{2,1,0:T(8,128)S(1)}) custom-call(f32[9,128,128]{2,1,0:T(8,128)S(1)} %get-tuple-element.27.map_part, f32[2,512,128]{2,1,0:T(8,128)S(1)} %get-tuple-element.28.fold_part, f32[9,96,128]{2,1,0:T(8,128)S(1)} %get-tuple-element.29.conv_part), custom_call_target="tpu_custom_call" | custom-call | tf_op jit(solution)/shard_map/pallas_call | solution.py:818
  128.9 0.7 copy.36
  129.6 0.8 copy.37
  130.4 0.9 copy.38
  131.3 0.8 copy.39
  132.1 0.8 copy.40
  (24 shorter events, 0.3 us)
Async XLA Ops:
  0.6 64.9 %copy-start.9 = (s32[3,4]{1,0:T(4,128)S(1)}, s32[3,4]{1,0:T(4,128)}, u32[]{:S(2)}) copy-start(s32[3,4]{1,0:T(4,128)} %coords.3) | copy-start | bytes 148
  3.0 1.0 copy-start
  4.0 0.9 copy-start.3
  4.9 0.9 copy-start.7
  5.9 0.7 copy-start.8
  6.6 33.3 %copy-start.5 = (bf16[48,32,128]{2,1,0:T(8,128)(2,1)S(1)}, bf16[48,32,128]{2,1,0:T(8,128)(2,1)}, u32[]{:S(2)}) copy-start(bf16[48,32,128]{2,1,0:T(8,128)(2,1)} %cot.1) | copy-start | bytes 1179652
  6.6 58.9 %copy-start.1 = (bf16[3,3,3,64,64]{4,3,2,1,0:T(8,128)(2,1)S(1)}, bf16[3,3,3,64,64]{4,3,2,1,0:T(8,128)(2,1)}, u32[]{:S(2)}) copy-start(bf16[3,3,3,64,64]{4,3,2,1,0:T(8,128)(2,1)} %param.13) | copy-start | bytes 663556
  6.6 58.9 %copy-start.4 = (bf16[1024,128]{1,0:T(8,128)(2,1)S(1)}, bf16[1024,128]{1,0:T(8,128)(2,1)}, u32[]{:S(2)}) copy-start(bf16[1024,128]{1,0:T(8,128)(2,1)} %param.15) | copy-start | bytes 786436
  38.4 1.0 copy-start.2
  39.9 1.0 copy-start.6
  40.9 0.7 copy-start.10
  41.5 0.7 copy-start.11
where the time goes:
time: 133 us
  Pallas kernels  118 us (89%)
  local copies, waits for them, and re-layouts  13.4 us (10%)
    pallas_call x1, Pallas kernels, body(): call(reduce_kernel, 4, [VMEM] * 3, [((9, 128, 128), F32), ((2, 512, 128),...  40.5 us
    pallas_call x1, Pallas kernels, body(): call(owner_forward, 1, [VMEM] * 5 + [SMEM] * 3, [((256, 512), F32), ((256...  31.8 us
    pallas_call x1, Pallas kernels, body(): call(map_kernel, 2, [VMEM, SMEM, SMEM, VMEM, VMEM, VMEM, VMEM], [((ROWS,...  23.3 us
    pallas_call x1, Pallas kernels, body(): call(owner_backward, 3, [VMEM] * 6 + [SMEM] * 3, [((NB, BS, BS, 512), F32...  22.9 us
    unnamed x30, local copies, waits for them, and re-layouts  11.7 us

commit v1 on v0

v1 whole, which is shorter than its diff:
```python
import functools

import jax
import jax.numpy as jnp
from jax import lax
from jax.experimental import pallas as pl
from jax.experimental.pallas import tpu as pltpu
from jax.sharding import PartitionSpec as P

MESH = pl.DeviceIdType.MESH
BF = jnp.bfloat16
F32 = jnp.float32
BS = 8
TR = 6
TC = 4
NB = 4
NX = 16
NY = 8
GROUP = NB * NY
ROWS = TR * BS
COLS = TC * BS
VMEM = pl.BlockSpec(memory_space=pltpu.VMEM)
SMEM = pl.BlockSpec(memory_space=pltpu.SMEM)
DMA = pltpu.SemaphoreType.DMA
CAT = 3072
CHUNK = CAT // NX
SLICE = CHUNK // NY


def place():
    return lax.axis_index("bx"), lax.axis_index("by")


def remote(src, dst, send, recv, device):
    return pltpu.make_async_remote_copy(
        src_ref=src,
        dst_ref=dst,
        send_sem=send,
        recv_sem=recv,
        device_id=device,
        device_id_type=MESH,
    )


def signal(device):
    pl.semaphore_signal(
        pltpu.get_barrier_semaphore(), inc=1, device_id=device, device_id_type=MESH
    )


def slope(pre):
    s = jax.nn.sigmoid(pre)
    return s * (1.0 + pre * (1.0 - s))


def rounded(v):
    return v.astype(BF).astype(F32)


def partners():
    bx, by = place()
    core = by % 2
    out = [(None, (bx, (by + k) % NY)) for k in range(1, NY)]
    out += [(None, ((bx + k) % NX, by)) for k in range(1, NX)]
    for step in (-1, 1):
        inside = bx > 0 if step < 0 else bx < NX - 1
        out += [(inside, (bx + step, core + 2 * j)) for j in range(NY // 2)]
        out.append((inside & (by > 0), (bx + step, by - 1)))
        out.append((inside & (by < NY - 1), (bx + step, by + 1)))
    return out


def greet():
    for ok, device in partners():
        if ok is None:
            signal(device)
        else:
            pl.when(ok)(functools.partial(signal, device))


def met():
    count = jnp.int32(0)
    for ok, _ in partners():
        count = count + (1 if ok is None else ok.astype(jnp.int32))
    pl.semaphore_wait(pltpu.get_barrier_semaphore(), count)


def pack_faces(cur, msg, coords):
    lane = lax.broadcasted_iota(jnp.int32, (32, 128), 1)

    def flat(v):
        return jnp.concatenate([v[:, t * 128 : (t + 1) * 128] for t in range(4)], 0)

    def one(n, carry):
        high = coords[2, n].astype(F32)
        msg[n, 0] = flat(cur[0, n]).astype(BF)
        msg[n, 1] = flat(cur[7, n]).astype(BF)
        msg[n, 2] = flat(cur[:, n, 0, :]).astype(BF)
        msg[n, 3] = flat(cur[:, n, 7, :]).astype(BF)
        top = cur[:, n, :, 384:512].reshape(64, 128)
        low = cur[:, n, :, 0:128].reshape(64, 128)
        face = pltpu.roll(top, 64, 1) * (1.0 - high) + low * high
        msg[n, 4] = jnp.where(lane < 64, face[0:32], pltpu.roll(face[32:64], 64, 1)).astype(BF)
        return carry

    lax.fori_loop(0, NB, one, 0)


class Faces:
    def __init__(self, msg, pool, side, own_s, fwd_s, side_s, sfwd_s, own_r, side_r):
        self.msg, self.pool, self.side = msg, pool, side
        self.own_s, self.fwd_s, self.side_s, self.sfwd_s = own_s, fwd_s, side_s, sfwd_s
        self.own_r, self.side_r = own_r, side_r
        self.bx, self.by = place()
        self.core = self.by % 2
        self.mate = self.by + 1 - 2 * self.core

    def first(self):
        bx, by = self.bx, self.by
        mine = pl.ds(by * NB, NB)
        out = [
            remote(self.msg, self.pool.at[mine], self.own_s.at[k], self.own_r.at[by], (bx, peer))
            for k, peer in enumerate([self.mate] + [(by + 2 * k) % NY for k in (1, 2, 3)])
        ]
        return out

    def sides(self, to):
        bx, by = self.bx, self.by
        mine = pl.ds(by * NB, NB)
        part, step = ((1, 1), (0, -1))[to]
        return [
            remote(
                self.msg.at[:, part],
                self.side.at[to, mine],
                self.side_s.at[to, j],
                self.side_r.at[to, by],
                (bx + step, self.core + 2 * j),
            )
            for j in range(4)
        ]

    def has(self, to):
        return (self.bx > 0, self.bx < NX - 1)[to]

    def sends(self, to):
        return self.has(1 - to)

    def start(self):
        for c in self.first():
            c.start()
        for to in range(2):

            @pl.when(self.sends(to))
            def _(to=to):
                for c in self.sides(to):
                    c.start()

        self.pool[pl.ds(self.by * NB, NB)] = self.msg[...]

    def own_landed(self, src, k):
        at = self.pool.at[pl.ds(src * NB, NB)]
        return remote(at, at, self.fwd_s.at[k], self.own_r.at[src], (self.bx, self.mate))

    def side_landed(self, to, src, j):
        at = self.side.at[to, pl.ds(src * NB, NB)]
        return remote(at, at, self.sfwd_s.at[to, j], self.side_r.at[to, src], (self.bx, self.mate))

    def forward(self):
        for k in (1, 3, 2):
            c = self.own_landed((self.by + 2 * k) % NY, k - 1)
            c.wait_recv()
            c.start()
        for to in range(2):

            @pl.when(self.has(to))
            def _(to=to):
                for j in range(4):
                    c = self.side_landed(to, self.core + 2 * j, j)
                    c.wait_recv()
                    c.start()

    def finish(self):
        for k in range(4):
            self.own_landed((self.mate + 2 * k) % NY, 0).wait_recv()
        for to in range(2):

            @pl.when(self.has(to))
            def _(to=to):
                for j in range(4):
                    self.side_landed(to, 1 - self.core + 2 * j, j).wait_recv()

    def drain(self):
        for c in self.first():
            c.wait_send()
        for k in (1, 2, 3):
            self.own_landed((self.by + 2 * k) % NY, k - 1).wait_send()
        for to in range(2):

            @pl.when(self.sends(to))
            def _(to=to):
                for c in self.sides(to):
                    c.wait_send()

            @pl.when(self.has(to))
            def _(to=to):
                for j in range(4):
                    self.side_landed(to, self.core + 2 * j, j).wait_send()


FACE_SCRATCH = [
    pltpu.VMEM((NB, 5, 32, 128), BF),
    pltpu.VMEM((GROUP + 1, 5, 32, 128), BF),
    pltpu.VMEM((2, GROUP + 1, 32, 128), BF),
    DMA((4,)),
    DMA((3,)),
    DMA((2, 4)),
    DMA((2, 4)),
    DMA((NY,)),
    DMA((2, NY)),
]


def assemble(cur, pool, side, neighbors, shifted, edge):
    low = lax.broadcasted_iota(jnp.int32, (8, 128), 1) < 64
    sub = lax.broadcasted_iota(jnp.int32, (8, 128), 0)

    bx, _ = place()

    def one(n, carry):
        def spot(k, group):
            at = neighbors[k, n]
            from_group = at - group * GROUP
            ok = (at >= 0) & (from_group >= 0) & (from_group < GROUP)
            return jnp.where(ok, from_group, GROUP)

        def face(part, k):
            return pool[spot(k, bx), part].astype(F32)

        def xface(dx, k):
            near = face(1 if dx < 0 else 0, k)
            return near + side[0 if dx < 0 else 1, spot(k, bx + dx)].astype(F32)

        def tiles(v):
            return [v[t * 8 : (t + 1) * 8] for t in range(4)]

        def turn(v):
            return pltpu.roll(v, 64, 1)

        def padz(core, before, after):
            r = [turn(t) for t in core]
            return (
                [jnp.where(low, before, r[0])]
                + [jnp.where(low, r[t - 1], r[t]) for t in (1, 2, 3)]
                + [jnp.where(low, r[3], after)]
            )

        def put(x, t, mid, above, below):
            row = pl.multiple_of((x * NB + n) * 8, 8)
            at = (pl.ds(row, 8), pl.ds(t * 128, 128))
            shifted[(1, *at)] = mid
            shifted[(0, *at)] = jnp.where(sub == 0, above, pltpu.roll(mid, 1, 0))
            shifted[(2, *at)] = jnp.where(sub == 7, below, pltpu.roll(mid, 7, 0))

        for x, dx in ((0, -1), (9, 1)):
            z = []
            for dy in range(3):
                k = 9 * (dx + 1) + 3 * dy
                z.append(
                    padz(tiles(xface(dx, k + 1)), turn(xface(dx, k)[24:32]), turn(xface(dx, k + 2)[0:8]))
                )
            for t in range(5):
                put(x, t, z[1][t], pltpu.roll(z[0][t], 1, 0), pltpu.roll(z[2][t], 7, 0))
        for i, (k, part) in enumerate(((9, 3), (15, 2))):
            z = padz(tiles(face(part, k + 1)), turn(face(part, k)[24:32]), turn(face(part, k + 2)[0:8]))
            for t in range(5):
                edge[i, :, t * 128 : (t + 1) * 128] = z[t]
        under = face(4, 12)
        over = face(4, 14)
        for x in range(BS):
            at = slice(x % 4 * 8, x % 4 * 8 + 8)
            before = under[at] if x < 4 else turn(under[at])
            after = turn(over[at]) if x < 4 else over[at]
            z = padz([cur[x, n, :, t * 128 : (t + 1) * 128] for t in range(4)], before, after)
            for t in range(5):
                lanes = slice(t * 128, (t + 1) * 128)
                put(x + 1, t, z[t], edge[0, x : x + 1, lanes], edge[1, x : x + 1, lanes])
        return carry

    lax.fori_loop(0, NB, one, 0)


NEAR = [(-1, 0), (1, 0), (0, -1), (0, 1), (-1, -1), (-1, 1), (1, -1), (1, 1)]


class Rim:
    def __init__(self, row_out, col_out, row_in, col_in, corner_in, send, recv):
        self.row_out, self.col_out = row_out, col_out
        self.row_in, self.col_in, self.corner_in = row_in, col_in, corner_in
        self.send, self.recv = send, recv
        self.bx, self.by = place()

    def exists(self, d):
        dx, dy = NEAR[d]
        ok = None
        for v, step, size in ((self.bx, dx, NX), (self.by, dy, NY)):
            if step:
                here = v > 0 if step < 0 else v < size - 1
                ok = here if ok is None else ok & here
        return ok

    def copy(self, d):
        dx, dy = NEAR[d]
        back = NEAR.index((-dx, -dy))
        if dy == 0:
            src, dst = self.row_out.at[d], self.row_in.at[back]
        elif dx == 0:
            src, dst = self.col_out.at[d - 2], self.col_in.at[back - 2]
        else:
            src = self.row_out.at[0 if dx < 0 else 1, pl.ds(0 if dy < 0 else 16, 16)]
            dst = self.corner_in.at[back - 4]
        return remote(src, dst, self.send.at[d], self.recv.at[back], (self.bx + dx, self.by + dy))

    def landing(self, d):
        dx, dy = NEAR[d]
        if dy == 0:
            return self.row_in.at[d]
        if dx == 0:
            return self.col_in.at[d - 2]
        return self.corner_in.at[d - 4]

    def start(self, plane):
        self.row_out[0] = plane[0].astype(BF)
        self.row_out[1] = plane[ROWS - 1].astype(BF)
        self.col_out[0] = plane[:, 0, :].astype(BF)
        self.col_out[1] = plane[:, COLS - 1, :].astype(BF)
        for d in range(8):

            @pl.when(self.exists(d))
            def _(d=d):
                self.copy(d).start()

            @pl.when(jnp.logical_not(self.exists(d)))
            def _(d=d):
                at = self.landing(d)
                at[...] = jnp.zeros(at.shape, BF)

    def finish(self):
        for d in range(8):

            @pl.when(self.exists(d))
            def _(d=d):
                dx, dy = NEAR[d]
                at = self.landing(d)
                remote(at, at, self.send.at[d], self.recv.at[d], (self.bx + dx, self.by + dy)).wait_recv()

    def drain(self):
        for d in range(8):

            @pl.when(self.exists(d))
            def _(d=d):
                self.copy(d).wait_send()


def spread(plane, rim, side32, out):
    side32[0] = rim.col_in[0].astype(F32)
    side32[1] = rim.col_in[1].astype(F32)
    j = lax.broadcasted_iota(jnp.int32, (COLS, 128), 0)

    def put(at, row, left, right):
        rows = pl.ds(pl.multiple_of(at * COLS, COLS), COLS)
        out[rows, 0:128] = jnp.where(j == 0, left, pltpu.roll(row, 1, 0)).astype(BF)
        out[rows, 128:256] = row.astype(BF)
        out[rows, 256:384] = jnp.where(j == COLS - 1, right, pltpu.roll(row, COLS - 1, 0)).astype(BF)

    def inner(i, carry):
        put(i + 1, plane[i], side32[0, pl.ds(i, 1), :], side32[1, pl.ds(i, 1), :])
        return carry

    lax.fori_loop(0, ROWS, inner, 0)
    corner = [rim.corner_in[c].astype(F32) for c in range(4)]
    put(0, rim.row_in[0].astype(F32), corner[0][15:16], corner[1][0:1])
    put(ROWS + 1, rim.row_in[1].astype(F32), corner[2][15:16], corner[3][0:1])

class Spread:
    def __init__(self, src, pool, size, own_s, fwd_s, own_r):
        self.src, self.pool, self.size = src, pool, size
        self.own_s, self.fwd_s, self.own_r = own_s, fwd_s, own_r
        self.bx, self.by = place()
        self.mate = self.by + 1 - 2 * (self.by % 2)

    def at(self, src):
        return self.pool.at[pl.ds(src * self.size, self.size)]

    def first(self):
        peers = [(self.by + 2) % NY, (self.by + 6) % NY, (self.by + 4) % NY, self.mate]
        return [
            remote(self.src, self.at(self.by), self.own_s.at[k], self.own_r.at[self.by], (self.bx, peer))
            for k, peer in enumerate(peers)
        ]

    def landed(self, src, k):
        at = self.at(src)
        return remote(at, at, self.fwd_s.at[k], self.own_r.at[src], (self.bx, self.mate))

    def start(self):
        for c in self.first():
            c.start()
        self.pool[pl.ds(self.by * self.size, self.size)] = self.src[...]

    def forward(self):
        for k in (1, 3, 2):
            c = self.landed((self.by + 2 * k) % NY, k - 1)
            c.wait_recv()
            c.start()

    def finish(self):
        for k in range(4):
            self.landed((self.mate + 2 * k) % NY, 0).wait_recv()

    def drain(self):
        for c in self.first():
            c.wait_send()
        for k in (1, 2, 3):
            self.landed((self.by + 2 * k) % NY, k - 1).wait_send()


def dot(a, b):
    return jnp.dot(a, b, preferred_element_type=F32)


def dot_t(a, b):
    return lax.dot_general(a, b, (((1,), (1,)), ((), ())), preferred_element_type=F32)


def window(wide, a, e, g):
    return wide[a * 32 : a * 32 + 256, e * 640 + g * 128 : e * 640 + g * 128 + 256]


def whole(
    vox_h, conv_w_h, fold_w_h, map_w_h, cot_h, conv_b, fold_b, map_b, coords, neighbors,
    bev_out, feat_out, conv_out, fold_out, map_out,
    vox, conv_w, fold_w, map_w, cot, load_sem,
    cur, shifted, edge, toep, toep_back, wide, pre, act, fold_both, part, part_pool,
    code, codes_v, codes, table,
    fold, plane, gplane, spread_mid, spread_grad, side32, slots, ready, back,
    split, cur_bf, cat, second, acc, third, summed, all32, chunk, fourth,
    face_a, face_f, part_sems, code_s, code_r, code_l,
    row_out, col_out, row_in, col_in, corner_in, rim_s, rim_r, back_s, back_r,
    zs, zr, ys, yr, gs, gr, ws, wr,
):
    bx, by = place()
    greet()
    loads = [
        pltpu.make_async_copy(src, dst, load_sem.at[i])
        for i, (src, dst) in enumerate(
            ((vox_h, vox), (conv_w_h, conv_w), (fold_w_h, fold_w), (map_w_h, map_w), (cot_h, cot))
        )
    ]
    for c in loads:
        c.start()
    lane = lax.broadcasted_iota(jnp.int32, (8, 128), 1)
    tile = jnp.zeros((8, 128), jnp.int32)
    for n in range(NB):
        number = ((coords[0, n] - bx * TR) * (TC * NY) + coords[1, n]) * 2 + coords[2, n]
        tile = jnp.where(lane == n, number, tile)
    code[...] = tile
    codes_v[by] = tile
    loads[0].wait()
    for n in range(NB):
        cur[:, n] = vox[n].astype(F32)
    faces = Faces(*face_a)
    pack_faces(cur, faces.msg, coords)
    met()
    tell = [
        remote(code, codes_v.at[by], code_s.at[k], code_r.at[by], (bx, (by + k) % NY)) for k in range(1, NY)
    ]
    for c in tell:
        c.start()
    faces.start()
    back_faces = Faces(*face_f)
    for f in (faces, back_faces):
        f.pool[GROUP] = jnp.zeros((5, 32, 128), BF)
        for to in range(2):
            f.side[to, GROUP] = jnp.zeros((32, 128), BF)
    loads[1].wait()
    blank = jnp.zeros((64, 64), F32)

    def build(tap, carry):
        w = [conv_w[tap * 3 + k].astype(F32) for k in range(3)]
        ahead = [blank, *w, blank]
        for z in range(4):
            toep[tap, z * 64 : (z + 1) * 64, :] = jnp.concatenate([ahead[z + 1], ahead[z]], 1).astype(BF)
        rows = ((w[2], w[1], w[0], blank), (blank, w[2], w[1], w[0]))
        for z in range(2):
            for half in range(2):
                pair = jnp.concatenate(rows[z][half * 2 : half * 2 + 2], 1)
                toep_back[tap, z * 64 : (z + 1) * 64, half * 128 : (half + 1) * 128] = pair.astype(BF)
        return carry

    lax.fori_loop(0, 9, build, 0)
    for k in range(1, NY):
        src = (by + k) % NY
        remote(code, codes_v.at[src], code_s.at[k], code_r.at[src], (bx, src)).wait_recv()
    to_scalar = pltpu.make_async_copy(codes_v.at[:, 0], codes, code_l.at[0])
    to_scalar.start()
    to_scalar.wait()

    def look(s, carry):
        want = ((s // (TC * 2)) * (TC * NY) + by * TC + (s // 2) % TC) * 2 + s % 2
        found = jnp.int32(GROUP)
        for b in range(GROUP):
            found = jnp.where(codes[b // NB, b % NB] == want, b, found)
        table[s] = found
        return carry

    lax.fori_loop(0, TR * TC * 2, look, 0)
    faces.forward()
    faces.finish()
    assemble(cur, faces.pool, faces.side, neighbors, shifted, edge)
    for e in range(3):
        wide[:, e * 640 : (e + 1) * 640] = shifted[e].astype(BF)
    for group in range(4):
        total = conv_b[...]
        for a in range(3):
            for e in range(3):
                total = total + dot(window(wide, a, e, group), toep[a * 3 + e])
        lanes = slice(group * 128, (group + 1) * 128)
        pre[:, lanes] = total
        act[:, lanes] = (total * jax.nn.sigmoid(total)).astype(BF)
    loads[2].wait()
    for h in range(2):
        fold_both[:, :, :, h * 128 : (h + 1) * 128] = dot(act[...], fold_w[h]).reshape(BS, NB, BS, 128)
    for n in range(NB):
        high = coords[2, n].astype(F32)
        one = fold_both[:, n, :, 0:128] * (1.0 - high) + fold_both[:, n, :, 128:256] * high
        part[n] = one.reshape(64, 128).astype(BF)
    parts = Spread(part, part_pool, NB, *part_sems)
    parts.start()
    loads[3].wait()
    loads[4].wait()
    parts.forward()
    parts.finish()

    rims = [
        Rim(row_out.at[p], col_out.at[p], row_in.at[p], col_in.at[p], corner_in.at[p], rim_s.at[p], rim_r.at[p])
        for p in range(2)
    ]
    for r in range(TR):
        for c in range(TC):
            total = fold_b[...]
            for h in range(2):
                at = table[(r * TC + c) * 2 + h]
                here = (at < GROUP).astype(F32)
                total = total + part_pool[jnp.minimum(at, GROUP - 1)].astype(F32) * here
            where = (slice(r * BS, (r + 1) * BS), slice(c * BS, (c + 1) * BS))
            fold[where] = total.reshape(BS, BS, 128)
            plane[where] = rounded(total * jax.nn.sigmoid(total)).reshape(BS, BS, 128)
    rims[0].start(plane)
    rims[0].finish()
    spread(plane, rims[0], side32, spread_mid)

    def ahead(i, carry):
        start = pl.multiple_of(i * 256, 256)
        total = map_b[...]
        for a in range(3):
            total = total + dot(spread_mid[pl.ds(start + a * COLS, 256), :], map_w[a])
        bev_out[pl.ds(i * BS, BS)] = (total * jax.nn.sigmoid(total)).reshape(BS, COLS, 128).astype(BF)
        g = cot[pl.ds(i * BS, BS)].astype(F32).reshape(256, 128) * slope(total)
        gplane[pl.ds(i * BS, BS)] = rounded(g).reshape(BS, COLS, 128)
        return carry

    lax.fori_loop(0, TR, ahead, 0)
    rims[1].start(gplane)
    turned = gplane[...].reshape(ROWS * COLS, 128).T.astype(BF)
    for a in range(3):
        got = dot(turned, spread_mid[a * COLS : a * COLS + ROWS * COLS, :])
        for e in range(3):
            t = a * 3 + e
            cat[t * 128 : (t + 1) * 128] = got[:, e * 128 : (e + 1) * 128].T.astype(BF)

    def gave(q):
        return remote(
            cat.at[pl.ds(q * CHUNK, CHUNK)], second.at[bx], zs.at[q], zr.at[bx], (q, by)
        )

    def give_chunks(qs):
        for q in qs:

            @pl.when(bx != q)
            def _(q=q):
                gave(q).start()

    give_chunks(range(6))
    rims[1].finish()
    spread(gplane, rims[1], side32, spread_grad)

    def behind(i, carry):
        start = pl.multiple_of(i * 256, 256)
        total = None
        for a in range(3):
            for e in range(3):
                lhs = spread_grad[pl.ds(start + a * COLS, 256), e * 128 : (e + 1) * 128]
                one = dot_t(lhs, map_w[2 - a, (2 - e) * 128 : (3 - e) * 128, :])
                total = one if total is None else total + one
        grad = (total * slope(fold[pl.ds(i * BS, BS)].reshape(256, 128))).reshape(BS, COLS, 128)
        for c in range(TC):
            slots[i * TC + c] = grad[:, c * BS : (c + 1) * BS, :].reshape(64, 128).astype(BF)
        return carry

    lax.fori_loop(0, TR, behind, 0)

    def fill(b, carry):
        number = codes[b // NB, b % NB] // 2
        c = number % (TC * NY) - by * TC
        at = number // (TC * NY) * TC + jnp.clip(c, 0, TC - 1)
        ready[b] = slots[jnp.clip(at, 0, TR * TC - 1)]
        return carry

    lax.fori_loop(0, GROUP, fill, 0)
    give = [
        remote(
            ready.at[pl.ds((by + k) % NY * NB, NB)],
            back.at[by],
            back_s.at[k],
            back_r.at[by],
            (bx, (by + k) % NY),
        )
        for k in (4, 3, 5, 2, 6, 1, 7)
    ]
    for c in give:
        c.start()
    back[by] = ready[pl.ds(by * NB, NB)]
    for k in range(1, NY):
        src = (by + k) % NY
        remote(ready.at[pl.ds(0, NB)], back.at[src], back_s.at[k], back_r.at[src], (bx, src)).wait_recv()

    for n in range(NB):
        high = coords[2, n].astype(F32)
        mine = back[jnp.clip(coords[1, n] // TC, 0, NY - 1), n].astype(F32).reshape(BS, BS, 128)
        split[:, n, :, 0:128] = mine * (1.0 - high)
        split[:, n, :, 128:256] = mine * high
    both = split[...].reshape(256, 256)
    act_grad = None
    for h in range(2):
        one = dot_t(both[:, h * 128 : (h + 1) * 128].astype(BF), fold_w[h])
        act_grad = one if act_grad is None else act_grad + one
    grad = rounded(rounded(act_grad) * slope(pre[...]))
    cur[...] = grad.reshape(BS, NB, BS, 512)
    cur_bf[...] = grad.astype(BF)
    pack_faces(cur, back_faces.msg, coords)
    back_faces.start()
    got = dot(both.T.astype(BF), act[...])
    for h in range(2):
        cat[1152 + h * 512 : 1152 + (h + 1) * 512] = got[h * 128 : (h + 1) * 128].T.astype(BF)
    give_chunks(range(6, 11))
    turned = [cur_bf[:, g * 128 : (g + 1) * 128].astype(F32).T.astype(BF) for g in range(4)]
    low = lax.broadcasted_iota(jnp.int32, (96, 128), 1) < 64
    for a in range(3):
        for e in range(3):
            total = None
            for g in range(4):
                one = dot(turned[g], window(wide, a, e, g))
                total = one if total is None else total + one
            total = total.T
            summed_z = total[0:192] + pltpu.roll(total[64:256], 64, 1)
            row = 2176 + (a * 3 + e) * 96
            cat[row : row + 96] = jnp.where(
                low, summed_z[0:96], pltpu.roll(summed_z[96:192], 64, 1)
            ).astype(BF)
    cat[3040:3072] = jnp.zeros((32, 128), BF)
    give_chunks(range(11, NX))
    acc[...] = cat[pl.ds(pl.multiple_of(bx * CHUNK, CHUNK), CHUNK)].astype(F32)
    for k in range(1, NX):
        src = (bx + k) % NX
        remote(cat.at[pl.ds(0, CHUNK)], second.at[src], zs.at[0], zr.at[src], (src, by)).wait_recv()
        acc[...] += second[src].astype(F32)

    def small(i):
        return pl.ds(pl.multiple_of(i * SLICE, SLICE), SLICE)

    def to_y(k, p):
        return remote(acc.at[small(p)], third.at[by], ys.at[k], yr.at[by], (bx, p))

    for k in range(1, NY):
        to_y(k, (by + k) % NY).start()
    back_faces.forward()
    total = acc[small(by)]
    for k in range(1, NY):
        src = (by + k) % NY
        remote(summed, third.at[src], ys.at[k], yr.at[src], (bx, src)).wait_recv()
        total = total + third[src]
    summed[...] = total
    all32[small(by)] = total

    def all_y(k, p):
        return remote(summed, all32.at[small(by)], gs.at[k], gr.at[by], (bx, p))

    for k in range(1, NY):
        all_y(k, (by + k) % NY).start()
    for k in range(1, NY):
        src = (by + k) % NY
        remote(summed, all32.at[small(src)], gs.at[k], gr.at[src], (bx, src)).wait_recv()
    chunk[...] = all32[...].astype(BF)

    def piece(i):
        return pl.ds(pl.multiple_of(i * CHUNK, CHUNK), CHUNK)

    def all_x(k):
        return remote(chunk, fourth.at[piece(bx)], ws.at[k], wr.at[bx], ((bx + k) % NX, by))

    for k in range(1, NX):
        all_x(k).start()
    fourth[piece(bx)] = chunk[...]
    back_faces.finish()
    assemble(cur, back_faces.pool, back_faces.side, neighbors, shifted, edge)
    for e in range(3):
        wide[:, e * 640 : (e + 1) * 640] = shifted[e].astype(BF)
    for g in range(4):
        total = None
        for a in range(3):
            for e in range(3):
                one = dot_t(window(wide, a, e, g), toep_back[(2 - a) * 3 + 2 - e])
                total = one if total is None else total + one
        view = total.reshape(BS, NB, BS, 128)
        for n in range(NB):
            feat_out[n, :, :, g * 128 : (g + 1) * 128] = view[:, n]
    for k in range(1, NX):
        src = (bx + k) % NX
        remote(chunk, fourth.at[piece(src)], ws.at[k], wr.at[src], (src, by)).wait_recv()
    for t in range(9):
        map_out[t] = fourth[t * 128 : (t + 1) * 128].astype(F32)
    for h in range(2):
        fold_out[h] = fourth[1152 + h * 512 : 1152 + (h + 1) * 512].astype(F32)
    for t in range(9):
        v = fourth[2176 + t * 96 : 2176 + (t + 1) * 96].astype(F32)
        conv_out[t, 0:96] = v[:, 0:64]
        conv_out[t, 96:192] = v[:, 64:128]

    for c in tell + give:
        c.wait_send()
    faces.drain()
    back_faces.drain()
    parts.drain()
    for rim in rims:
        rim.drain()
    for q in range(NX):

        @pl.when(bx != q)
        def _(q=q):
            gave(q).wait_send()

    for k in range(1, NY):
        to_y(k, (by + k) % NY).wait_send()
        all_y(k, (by + k) % NY).wait_send()
    for k in range(1, NX):
        all_x(k).wait_send()


def body(vox_feats, block_coords, neighbors, conv_w, conv_b, fold_w, fold_b, map_w, map_b, cotangent):
    far = pl.BlockSpec(memory_space=pl.ANY)
    bev_map, feat_grad, conv_grads, fold_grads, map_grads = pl.pallas_call(
        whole,
        in_specs=[far] * 5 + [VMEM] * 3 + [SMEM] * 2,
        out_specs=[VMEM] * 5,
        out_shape=[
            jax.ShapeDtypeStruct((ROWS, COLS, 128), BF),
            jax.ShapeDtypeStruct((NB, BS, BS, 512), F32),
            jax.ShapeDtypeStruct((9, 192, 64), F32),
            jax.ShapeDtypeStruct((2, 512, 128), F32),
            jax.ShapeDtypeStruct((9, 128, 128), F32),
        ],
        scratch_shapes=[
            pltpu.VMEM((NB, BS, BS, 512), BF),
            pltpu.VMEM((27, 64, 64), BF),
            pltpu.VMEM((2, 512, 128), BF),
            pltpu.VMEM((3, 384, 128), BF),
            pltpu.VMEM((ROWS, COLS, 128), BF),
            DMA((5,)),
            pltpu.VMEM((BS, NB, BS, 512), F32),
            pltpu.VMEM((3, 320, 640), F32),
            pltpu.VMEM((2, 8, 640), F32),
            pltpu.VMEM((9, 256, 128), BF),
            pltpu.VMEM((9, 128, 256), BF),
            pltpu.VMEM((320, 1920), BF),
            pltpu.VMEM((256, 512), F32),
            pltpu.VMEM((256, 512), BF),
            pltpu.VMEM((BS, NB, BS, 256), F32),
            pltpu.VMEM((NB, 64, 128), BF),
            pltpu.VMEM((GROUP, 64, 128), BF),
            pltpu.VMEM((8, 128), jnp.int32),
            pltpu.VMEM((NY, 8, 128), jnp.int32),
            pltpu.SMEM((NY, 128), jnp.int32),
            pltpu.SMEM((TR * TC * 2,), jnp.int32),
            pltpu.VMEM((ROWS, COLS, 128), F32),
            pltpu.VMEM((ROWS, COLS, 128), F32),
            pltpu.VMEM((ROWS, COLS, 128), F32),
            pltpu.VMEM(((ROWS + 2) * COLS, 384), BF),
            pltpu.VMEM(((ROWS + 2) * COLS, 384), BF),
            pltpu.VMEM((2, ROWS, 128), F32),
            pltpu.VMEM((TR * TC, 64, 128), BF),
            pltpu.VMEM((GROUP, 64, 128), BF),
            pltpu.VMEM((NY, NB, 64, 128), BF),
            pltpu.VMEM((BS, NB, BS, 256), F32),
            pltpu.VMEM((256, 512), BF),
            pltpu.VMEM((CAT, 128), BF),
            pltpu.VMEM((NX, CHUNK, 128), BF),
            pltpu.VMEM((CHUNK, 128), F32),
            pltpu.VMEM((NY, SLICE, 128), F32),
            pltpu.VMEM((SLICE, 128), F32),
            pltpu.VMEM((CHUNK, 128), F32),
            pltpu.VMEM((CHUNK, 128), BF),
            pltpu.VMEM((CAT, 128), BF),
            FACE_SCRATCH,
            FACE_SCRATCH,
            [DMA((4,)), DMA((3,)), DMA((NY,))],
            DMA((NY,)),
            DMA((NY,)),
            DMA((1,)),
            pltpu.VMEM((2, 2, COLS, 128), BF),
            pltpu.VMEM((2, 2, ROWS, 128), BF),
            pltpu.VMEM((2, 2, COLS, 128), BF),
            pltpu.VMEM((2, 2, ROWS, 128), BF),
            pltpu.VMEM((2, 4, 16, 128), BF),
            DMA((2, 8)),
            DMA((2, 8)),
            DMA((NY,)),
            DMA((NY,)),
            DMA((NX,)),
            DMA((NX,)),
            DMA((NY,)),
            DMA((NY,)),
            DMA((NY,)),
            DMA((NY,)),
            DMA((NX,)),
            DMA((NX,)),
        ],
        compiler_params=pltpu.CompilerParams(
            collective_id=1, has_side_effects=True, vmem_limit_bytes=58 * 2**20
        ),
    )(
        vox_feats,
        conv_w.reshape(27, 64, 64),
        fold_w.reshape(2, 512, 128),
        map_w.reshape(3, 384, 128),
        cotangent,
        jnp.concatenate([conv_b, conv_b])[None],
        fold_b[None],
        map_b[None],
        block_coords,
        neighbors,
    )
    return (
        bev_map,
        feat_grad,
        conv_grads.reshape(3, 3, 3, 64, 64),
        fold_grads.reshape(1024, 128),
        map_grads.reshape(3, 3, 128, 128),
    )


def solution(mesh):
    placed = (
        P(("bx", "by"), None, None, None),
        P(None, ("bx", "by")),
        P(None, ("bx", "by")),
        P(),
        P(),
        P(),
        P(),
        P(),
        P(),
        P("bx", "by", None),
    )
    return jax.shard_map(
        body,
        mesh=mesh,
        in_specs=placed,
        out_specs=(P("bx", "by", None), P(("bx", "by"), None, None, None), P(), P(), P()),
        check_vma=False,
    )
```

time: 133 us -> 98.5 us (0.74)
  Pallas kernels: 118 us -> 89.3 us
  local copies, waits for them, and re-layouts: 13.4 us -> 7.44 us
    pallas_call x4 -> x1, Pallas kernels: 118 us -> 89.3 us  [body(): pl.pallas_call(whole, in_specs=[far] * 5 + [VMEM] * 3 + [SMEM] * 2, out_s...]
    unnamed x30 -> x18, local copies, waits for them, and re-layouts: 11.7 us -> 7.44 us
where the time goes in v1:
time: 98.5 us; the launch traced here: 98 us
  Pallas kernels  89.3 us (91%)
  local copies, waits for them, and re-layouts  7.44 us (8%)
    pallas_call x1, Pallas kernels, body(): pl.pallas_call(whole, in_specs=[far] * 5 + [VMEM] * 3 + [SMEM] * 2, out_s...  89.3 us
    unnamed x18, local copies, waits for them, and re-layouts  7.44 us

profile of v1, /device:TPU:1, one launch (start us, length us, event | category | flops | bytes accessed | tf_op | source)
XLA Modules:
  0.0 98.0 jit_solution(3633796186908095404)
XLA Ops:
  0.6 0.0 copy-start.5
  0.6 0.0 copy-start.4
  0.7 0.6 copy-done.5
  1.3 0.6 maximum_bitcast_fusion.conv_b
  1.9 0.0 copy-done.4
  1.9 0.7 copy.15.neighbors
  2.6 89.3 %shard_map.137 = (bf16[48,32,128]{2,1,0:T(8,128)(2,1)}, f32[4,8,8,512]{3,2,1,0:T(8,128)}, f32[9,192,64]{2,1,0:T(8,128)}, f32[2,512,128]{2,1,0:T(8,128)}, f32[9,128,128]{2,1,0:T(8,128)}) custom-call(bf16[4,8,8,512]{3,2,1,0:T(8,128)(2,1)} %vox_h.1, bf16[27,64,64]{2,1,0:T(8,128)(2,1)} %bitcast.13, bf16[2,512,128]{2,1,0:T(8,128)(2,1)} %bitcast.15, ...), custom_call_target="tpu_custom_call" | custom-call | tf_op jit(solution)/shard_map/pallas_call | solution.py:761
  91.9 0.0 copy-start.3
  91.9 0.0 copy-start
  91.9 1.9 %copy.21 = bf16[48,32,128]{2,1,0:T(8,128)(2,1)} copy(bf16[48,32,128]{2,1,0:T(8,128)(2,1)} %get-tuple-element.20) | data formatting | bytes 786432
  93.8 0.0 copy-done.3
  93.8 0.8 copy.22
  94.6 0.0 copy-done
  94.6 0.0 copy-start.2
  94.6 0.9 copy.23
  95.5 0.4 copy-done.2
  96.0 0.0 copy-start.1
  96.0 0.8 copy.24
  96.8 0.5 copy-done.1
  97.2 0.8 copy.25
Async XLA Ops:
  0.6 0.7 copy-start.5
  0.6 1.2 %copy-start.4 = (s32[27,4]{0,1:T(4,128)S(1)}, s32[27,4]{0,1:T(4,128)}, u32[]{:S(2)}) copy-start(s32[27,4]{0,1:T(4,128)} %param.12) | copy-start | bytes 1300
  91.9 1.9 %copy-start.3 = (f32[4,8,8,512]{3,2,1,0:T(8,128)S(1)}, f32[4,8,8,512]{3,2,1,0:T(8,128)}, u32[]{:S(2)}) copy-start(f32[4,8,8,512]{3,2,1,0:T(8,128)} %get-tuple-element.21) | copy-start | bytes 1572868
  91.9 2.7 %copy-start = (f32[9,192,64]{2,1,0:T(8,128)S(1)}, f32[9,192,64]{2,1,0:T(8,128)}, u32[]{:S(2)}) copy-start(f32[9,192,64]{2,1,0:T(8,128)} %get-tuple-element.12) | copy-start | bytes 1327108
  94.6 1.4 %copy-start.2 = (f32[2,512,128]{2,1,0:T(8,128)S(1)}, f32[2,512,128]{2,1,0:T(8,128)}, u32[]{:S(2)}) copy-start(f32[2,512,128]{2,1,0:T(8,128)} %get-tuple-element.13) | copy-start | bytes 1572868
  96.0 1.3 %copy-start.1 = (f32[9,128,128]{2,1,0:T(8,128)S(1)}, f32[9,128,128]{2,1,0:T(8,128)}, u32[]{:S(2)}) copy-start(f32[9,128,128]{2,1,0:T(8,128)} %get-tuple-element.14) | copy-start | bytes 1769476

commit v2 on v1

--- a/solution.py
+++ b/solution.py
@@ -23,8 +23,6 @@
 SMEM = pl.BlockSpec(memory_space=pltpu.SMEM)
 DMA = pltpu.SemaphoreType.DMA
 CAT = 3072
-CHUNK = CAT // NX
-SLICE = CHUNK // NY
 
 
 def place():
@@ -228,7 +226,7 @@
 
     def one(n, carry):
         def spot(k, group):
-            at = neighbors[k, n]
+            at = neighbors[n, k]
             from_group = at - group * GROUP
             ok = (at >= 0) & (from_group >= 0) & (from_group < GROUP)
             return jnp.where(ok, from_group, GROUP)
@@ -424,6 +422,119 @@
             self.landed((self.by + 2 * k) % NY, k - 1).wait_send()
 
 
+class Total:
+    def __init__(self, base, half, cat, given, sums, second, ring, full, ms, mr, zs, zr, xs, xr, ws, wr, fs, fr):
+        self.base, self.half, self.chunk = base, half, half // NX
+        self.cat, self.given, self.sums, self.second = cat, given, sums, second
+        self.ring, self.full = ring, full
+        self.ms, self.mr, self.zs, self.zr, self.xs, self.xr = ms, mr, zs, zr, xs, xr
+        self.ws, self.wr, self.fs, self.fr = ws, wr, fs, fr
+        self.bx, self.by = place()
+        self.core = self.by % 2
+        self.mate = self.by + 1 - 2 * self.core
+        self.chip = self.by // 2
+
+    def rows(self, core):
+        return pl.ds(pl.multiple_of(self.base + core * self.half, self.half), self.half)
+
+    def piece(self, core, i):
+        return pl.ds(pl.multiple_of(core * self.half + i * self.chunk, self.chunk), self.chunk)
+
+    def to_mate(self):
+        at = self.cat.at[self.rows(1 - self.core)]
+        return remote(at, self.given, self.ms.at[0], self.mr.at[0], (self.bx, self.mate))
+
+    def to_x(self, q):
+        at = self.sums.at[pl.ds(q * self.chunk, self.chunk)]
+        return remote(at, self.second.at[self.bx], self.zs.at[q], self.zr.at[self.bx], (q, self.by))
+
+    def combine(self):
+        self.to_mate().wait_recv()
+        self.sums[...] = (self.cat[self.rows(self.core)].astype(F32) + self.given[...].astype(F32)).astype(BF)
+        for q in range(NX):
+
+            @pl.when(self.bx != q)
+            def _(q=q):
+                self.to_x(q).start()
+
+    def to_ring(self, k):
+        at = self.ring.at[self.chip]
+        to = (self.by + 2 * k) % NY
+        return remote(at, at, self.xs.at[k], self.xr.at[self.chip], (self.bx, to))
+
+    def sum_x(self):
+        mine = pl.ds(pl.multiple_of(self.bx * self.chunk, self.chunk), self.chunk)
+        total = self.sums[mine].astype(F32)
+        for k in range(1, NX):
+            src = (self.bx + k) % NX
+            at = self.second.at[src]
+            remote(at, at, self.zs.at[0], self.zr.at[src], (src, self.by)).wait_recv()
+            total = total + self.second[src].astype(F32)
+        self.ring[self.chip] = total.astype(BF)
+        for k in (1, 3, 2):
+            self.to_ring(k).start()
+
+    def out_x(self, k):
+        at = self.full.at[self.piece(self.core, self.bx)]
+        return remote(at, at, self.ws.at[k], self.wr.at[self.bx], ((self.bx + k) % NX, self.by))
+
+    def pass_on(self, src):
+        at = self.full.at[self.piece(self.core, src)]
+        return remote(at, at, self.fs.at[src], self.fr.at[src], (self.bx, self.mate))
+
+    def sum_ring(self):
+        for k in range(1, 4):
+            src = (self.chip + k) % 4
+            at = self.ring.at[src]
+            remote(at, at, self.xs.at[k], self.xr.at[src], (self.bx, src * 2 + self.core)).wait_recv()
+        total = self.ring[0].astype(F32)
+        for i in range(1, 4):
+            total = total + self.ring[i].astype(F32)
+        self.full[self.piece(self.core, self.bx)] = total.astype(BF)
+        for k in range(1, NX):
+            self.out_x(k).start()
+        self.pass_on(self.bx).start()
+
+    def relay(self):
+        for k in range(1, NX):
+            src = (self.bx + k) % NX
+            at = self.full.at[self.piece(self.core, src)]
+            remote(at, at, self.ws.at[k], self.wr.at[src], (src, self.by)).wait_recv()
+            self.pass_on(src).start()
+
+    def done(self):
+        for src in range(NX):
+            at = self.full.at[self.piece(1 - self.core, src)]
+            remote(at, at, self.fs.at[src], self.fr.at[src], (self.bx, self.mate)).wait_recv()
+
+    def drain(self):
+        self.to_mate().wait_send()
+        for q in range(NX):
+
+            @pl.when(self.bx != q)
+            def _(q=q):
+                self.to_x(q).wait_send()
+
+        for k in range(1, 4):
+            self.to_ring(k).wait_send()
+        for k in range(1, NX):
+            self.out_x(k).wait_send()
+        for src in range(NX):
+            self.pass_on(src).wait_send()
+
+
+def total_scratch(half):
+    chunk = half // NX
+    return [
+        pltpu.VMEM((half, 128), BF),
+        pltpu.VMEM((half, 128), BF),
+        pltpu.VMEM((NX, chunk, 128), BF),
+        pltpu.VMEM((4, chunk, 128), BF),
+        pltpu.VMEM((2 * half, 128), BF),
+        *[DMA((n,)) for n in (1, 1, NX, NX, 4, 4, NX, NX, NX, NX)],
+    ]
+
+
 def dot(a, b):
     return jnp.dot(a, b, preferred_element_type=F32)
 
@@ -438,18 +549,27 @@
 
 def whole(
     vox_h, conv_w_h, fold_w_h, map_w_h, cot_h, conv_b, fold_b, map_b, coords, neighbors,
-    bev_out, feat_out, conv_out, fold_out, map_out,
+    bev_far, feat_far, conv_far, fold_far, map_far,
+    bev_out, feat_out, conv_out, fold_out, map_out, out_sem,
     vox, conv_w, fold_w, map_w, cot, load_sem,
     cur, shifted, edge, toep, toep_back, wide, pre, act, fold_both, part, part_pool,
     code, codes_v, codes, table,
     fold, plane, gplane, spread_mid, spread_grad, side32, slots, ready, back,
-    split, cur_bf, cat, second, acc, third, summed, all32, chunk, fourth,
+    split, cur_bf, cat, early_part, late_part,
     face_a, face_f, part_sems, code_s, code_r, code_l,
     row_out, col_out, row_in, col_in, corner_in, rim_s, rim_r, back_s, back_r,
-    zs, zr, ys, yr, gs, gr, ws, wr,
 ):
     bx, by = place()
     greet()
+    stores = [
+        pltpu.make_async_copy(src, dst, out_sem.at[i])
+        for i, (src, dst) in enumerate(
+            ((bev_out, bev_far), (feat_out, feat_far), (conv_out, conv_far), (fold_out, fold_far), (map_out, map_far))
+        )
+    ]
+    early = Total(0, 1024, cat, *early_part)
+    late = Total(2048, 512, cat, *late_part)
+    core = by % 2
     loads = [
         pltpu.make_async_copy(src, dst, load_sem.at[i])
         for i, (src, dst) in enumerate(
@@ -520,7 +640,7 @@
     for e in range(3):
         wide[:, e * 640 : (e + 1) * 640] = shifted[e].astype(BF)
     for group in range(4):
-        total = conv_b[...]
+        total = jnp.concatenate([conv_b[...], conv_b[...]], 1)
         for a in range(3):
             for e in range(3):
                 total = total + dot(window(wide, a, e, group), toep[a * 3 + e])
@@ -570,27 +690,21 @@
         return carry
 
     lax.fori_loop(0, TR, ahead, 0)
+    stores[0].start()
     rims[1].start(gplane)
     turned = gplane[...].reshape(ROWS * COLS, 128).T.astype(BF)
     for a in range(3):
         got = dot(turned, spread_mid[a * COLS : a * COLS + ROWS * COLS, :])
         for e in range(3):
             t = a * 3 + e
-            cat[t * 128 : (t + 1) * 128] = got[:, e * 128 : (e + 1) * 128].T.astype(BF)
-
-    def gave(q):
-        return remote(
-            cat.at[pl.ds(q * CHUNK, CHUNK)], second.at[bx], zs.at[q], zr.at[bx], (q, by)
-        )
-
-    def give_chunks(qs):
-        for q in qs:
-
-            @pl.when(bx != q)
-            def _(q=q):
-                gave(q).start()
-
-    give_chunks(range(6))
+            row = t * 128 if t < 8 else 2048
+            cat[row : row + 128] = got[:, e * 128 : (e + 1) * 128].T.astype(BF)
+
+
+    @pl.when(core == 1)
+    def _():
+        early.to_mate().start()
+
     rims[1].finish()
     spread(gplane, rims[1], side32, spread_grad)
 
@@ -630,6 +744,7 @@
     for c in give:
         c.start()
     back[by] = ready[pl.ds(by * NB, NB)]
+    pl.when(core == 0)(early.combine)
     for k in range(1, NY):
         src = (by + k) % NY
         remote(ready.at[pl.ds(0, NB)], back.at[src], back_s.at[k], back_r.at[src], (bx, src)).wait_recv()
@@ -651,8 +766,12 @@
     back_faces.start()
     got = dot(both.T.astype(BF), act[...])
     for h in range(2):
-        cat[1152 + h * 512 : 1152 + (h + 1) * 512] = got[h * 128 : (h + 1) * 128].T.astype(BF)
-    give_chunks(range(6, 11))
+        cat[1024 + h * 512 : 1024 + (h + 1) * 512] = got[h * 128 : (h + 1) * 128].T.astype(BF)
+
+    @pl.when(core == 0)
+    def _():
+        early.to_mate().start()
+
     turned = [cur_bf[:, g * 128 : (g + 1) * 128].astype(F32).T.astype(BF) for g in range(4)]
     low = lax.broadcasted_iota(jnp.int32, (96, 128), 1) < 64
     for a in range(3):
@@ -668,49 +787,14 @@
                 low, summed_z[0:96], pltpu.roll(summed_z[96:192], 64, 1)
             ).astype(BF)
     cat[3040:3072] = jnp.zeros((32, 128), BF)
-    give_chunks(range(11, NX))
-    acc[...] = cat[pl.ds(pl.multiple_of(bx * CHUNK, CHUNK), CHUNK)].astype(F32)
-    for k in range(1, NX):
-        src = (bx + k) % NX
-        remote(cat.at[pl.ds(0, CHUNK)], second.at[src], zs.at[0], zr.at[src], (src, by)).wait_recv()
-        acc[...] += second[src].astype(F32)
-
-    def small(i):
-        return pl.ds(pl.multiple_of(i * SLICE, SLICE), SLICE)
-
-    def to_y(k, p):
-        return remote(acc.at[small(p)], third.at[by], ys.at[k], yr.at[by], (bx, p))
-
-    for k in range(1, NY):
-        to_y(k, (by + k) % NY).start()
+    late.to_mate().start()
+    pl.when(core == 1)(early.combine)
+    late.combine()
+    early.sum_x()
+    late.sum_x()
+    early.sum_ring()
     back_faces.forward()
-    total = acc[small(by)]
-    for k in range(1, NY):
-        src = (by + k) % NY
-        remote(summed, third.at[src], ys.at[k], yr.at[src], (bx, src)).wait_recv()
-        total = total + third[src]
-    summed[...] = total
-    all32[small(by)] = total
-
-    def all_y(k, p):
-        return remote(summed, all32.at[small(by)], gs.at[k], gr.at[by], (bx, p))
-
-    for k in range(1, NY):
-        all_y(k, (by + k) % NY).start()
-    for k in range(1, NY):
-        src = (by + k) % NY
-        remote(summed, all32.at[small(src)], gs.at[k], gr.at[src], (bx, src)).wait_recv()
-    chunk[...] = all32[...].astype(BF)
-
-    def piece(i):
-        return pl.ds(pl.multiple_of(i * CHUNK, CHUNK), CHUNK)
-
-    def all_x(k):
-        return remote(chunk, fourth.at[piece(bx)], ws.at[k], wr.at[bx], ((bx + k) % NX, by))
-
-    for k in range(1, NX):
-        all_x(k).start()
-    fourth[piece(bx)] = chunk[...]
+    late.sum_ring()
     back_faces.finish()
     assemble(cur, back_faces.pool, back_faces.side, neighbors, shifted, edge)
     for e in range(3):
@@ -724,17 +808,23 @@
         view = total.reshape(BS, NB, BS, 128)
         for n in range(NB):
             feat_out[n, :, :, g * 128 : (g + 1) * 128] = view[:, n]
-    for k in range(1, NX):
-        src = (bx + k) % NX
-        remote(chunk, fourth.at[piece(src)], ws.at[k], wr.at[src], (src, by)).wait_recv()
+    stores[1].start()
+    early.relay()
+    late.relay()
+    early.done()
+    for h in range(2):
+        fold_out[h] = early.full[1024 + h * 512 : 1024 + (h + 1) * 512].astype(F32)
+    stores[3].start()
+    for t in range(8):
+        map_out[t] = early.full[t * 128 : (t + 1) * 128].astype(F32)
+    late.done()
+    map_out[8] = late.full[0:128].astype(F32)
+    stores[4].start()
     for t in range(9):
-        map_out[t] = fourth[t * 128 : (t + 1) * 128].astype(F32)
-    for h in range(2):
-        fold_out[h] = fourth[1152 + h * 512 : 1152 + (h + 1) * 512].astype(F32)
-    for t in range(9):
-        v = fourth[2176 + t * 96 : 2176 + (t + 1) * 96].astype(F32)
+        v = late.full[128 + t * 96 : 128 + (t + 1) * 96].astype(F32)
         conv_out[t, 0:96] = v[:, 0:64]
         conv_out[t, 96:192] = v[:, 64:128]
+    stores[2].start()
 
     for c in tell + give:
         c.wait_send()
@@ -743,33 +833,42 @@
     parts.drain()
     for rim in rims:
         rim.drain()
-    for q in range(NX):
-
-        @pl.when(bx != q)
-        def _(q=q):
-            gave(q).wait_send()
-
-    for k in range(1, NY):
-        to_y(k, (by + k) % NY).wait_send()
-        all_y(k, (by + k) % NY).wait_send()
-    for k in range(1, NX):
-        all_x(k).wait_send()
+    early.drain()
+    late.drain()
+    for c in stores:
+        c.wait()
+
+
+def hand_on(*refs):
+    given, results, held, sems = refs[:5], refs[5:10], refs[10:15], refs[15]
+    takes = [pltpu.make_async_copy(a, b, sems.at[0, i]) for i, (a, b) in enumerate(zip(given, held, strict=True))]
+    gives = [pltpu.make_async_copy(a, b, sems.at[1, i]) for i, (a, b) in enumerate(zip(held, results, strict=True))]
+    for c in takes:
+        c.start()
+    for take, give in zip(takes, gives, strict=True):
+        take.wait()
+        give.start()
+    for c in gives:
+        c.wait()
 
 
 def body(vox_feats, block_coords, neighbors, conv_w, conv_b, fold_w, fold_b, map_w, map_b, cotangent):
     far = pl.BlockSpec(memory_space=pl.ANY)
-    bev_map, feat_grad, conv_grads, fold_grads, map_grads = pl.pallas_call(
+    outs = [
+        jax.ShapeDtypeStruct((ROWS, COLS, 128), BF),
+        jax.ShapeDtypeStruct((NB, BS, BS, 512), F32),
+        jax.ShapeDtypeStruct((9, 192, 64), F32),
+        jax.ShapeDtypeStruct((2, 512, 128), F32),
+        jax.ShapeDtypeStruct((9, 128, 128), F32),
+    ]
+    made = pl.pallas_call(
         whole,
         in_specs=[far] * 5 + [VMEM] * 3 + [SMEM] * 2,
-        out_specs=[VMEM] * 5,
-        out_shape=[
-            jax.ShapeDtypeStruct((ROWS, COLS, 128), BF),
-            jax.ShapeDtypeStruct((NB, BS, BS, 512), F32),
-            jax.ShapeDtypeStruct((9, 192, 64), F32),
-            jax.ShapeDtypeStruct((2, 512, 128), F32),
-            jax.ShapeDtypeStruct((9, 128, 128), F32),
-        ],
+        out_specs=[far] * 5,
+        out_shape=outs,
         scratch_shapes=[
+            *[pltpu.VMEM(o.shape, o.dtype) for o in outs],
+            DMA((5,)),
             pltpu.VMEM((NB, BS, BS, 512), BF),
             pltpu.VMEM((27, 64, 64), BF),
             pltpu.VMEM((2, 512, 128), BF),
@@ -803,13 +902,8 @@
             pltpu.VMEM((BS, NB, BS, 256), F32),
             pltpu.VMEM((256, 512), BF),
             pltpu.VMEM((CAT, 128), BF),
-            pltpu.VMEM((NX, CHUNK, 128), BF),
-            pltpu.VMEM((CHUNK, 128), F32),
-            pltpu.VMEM((NY, SLICE, 128), F32),
-            pltpu.VMEM((SLICE, 128), F32),
-            pltpu.VMEM((CHUNK, 128), F32),
-            pltpu.VMEM((CHUNK, 128), BF),
-            pltpu.VMEM((CAT, 128), BF),
+            total_scratch(1024),
+            total_scratch(512),
             FACE_SCRATCH,
             FACE_SCRATCH,
             [DMA((4,)), DMA((3,)), DMA((NY,))],
@@ -825,14 +919,6 @@
             DMA((2, 8)),
             DMA((NY,)),
             DMA((NY,)),
-            DMA((NX,)),
-            DMA((NX,)),
-            DMA((NY,)),
-            DMA((NY,)),
-            DMA((NY,)),
-            DMA((NY,)),
-            DMA((NX,)),
-            DMA((NX,)),
         ],
         compiler_params=pltpu.CompilerParams(
             collective_id=1, has_side_effects=True, vmem_limit_bytes=58 * 2**20
@@ -843,12 +929,20 @@
         fold_w.reshape(2, 512, 128),
         map_w.reshape(3, 384, 128),
         cotangent,
-        jnp.concatenate([conv_b, conv_b])[None],
+        conv_b[None],
         fold_b[None],
         map_b[None],
         block_coords,
-        neighbors,
+        neighbors.T,
     )
+    bev_map, feat_grad, conv_grads, fold_grads, map_grads = pl.pallas_call(
+        hand_on,
+        in_specs=[far] * 5,
+        out_specs=[far] * 5,
+        out_shape=outs,
+        scratch_shapes=[*[pltpu.VMEM(o.shape, o.dtype) for o in outs], DMA((2, 5))],
+        compiler_params=pltpu.CompilerParams(vmem_limit_bytes=58 * 2**20),
+    )(*made)
     return (
         bev_map,
         feat_grad,

time: 98.5 us -> 85.7 us (0.87)
  local copies, waits for them, and re-layouts: 7.44 us -> 0 us
  Pallas kernels: 89.3 us -> 84.9 us
    unnamed x18 -> x0, local copies, waits for them, and re-layouts: 7.44 us -> none
    pallas_call x1, Pallas kernels: 89.3 us -> 82 us  [body(): pl.pallas_call(whole, in_specs=[far] * 5 + [VMEM] * 3 + [SMEM] * 2, out_s...]
    pallas_call x0 -> x1, Pallas kernels: none -> 2.82 us  [body(): pl.pallas_call(hand_on, in_specs=[far] * 5, out_specs=[far] * 5, out_shap...]
where the time goes in v2:
time: 85.7 us; the launch traced here: 85.5 us
  Pallas kernels  84.9 us (99%)
    pallas_call x1, Pallas kernels, body(): pl.pallas_call(whole, in_specs=[far] * 5 + [VMEM] * 3 + [SMEM] * 2, out_s...  82 us
    pallas_call x1, Pallas kernels, body(): pl.pallas_call(hand_on, in_specs=[far] * 5, out_specs=[far] * 5, out_shap...  2.82 us

profile of v2, /device:TPU:1, one launch (start us, length us, event | category | flops | bytes accessed | tf_op | source)
XLA Modules:
  0.0 85.5 jit_solution(4368258504821198689)
XLA Ops:
  0.6 82.0 %shard_map.137 = (bf16[48,32,128]{2,1,0:T(8,128)(2,1)}, f32[4,8,8,512]{3,2,1,0:T(8,128)}, f32[9,192,64]{2,1,0:T(8,128)}, f32[2,512,128]{2,1,0:T(8,128)}, f32[9,128,128]{2,1,0:T(8,128)}) custom-call(bf16[4,8,8,512]{3,2,1,0:T(8,128)(2,1)} %vox_h.1, bf16[27,64,64]{2,1,0:T(8,128)(2,1)} %bitcast.10, bf16[2,512,128]{2,1,0:T(8,128)(2,1)} %bitcast.12, ...), custom_call_target="tpu_custom_call" | custom-call | tf_op jit(solution)/shard_map/pallas_call | solution.py:864
  82.7 2.8 %shard_map.138 = (bf16[48,32,128]{2,1,0:T(8,128)(2,1)}, f32[4,8,8,512]{3,2,1,0:T(8,128)}, f32[9,192,64]{2,1,0:T(8,128)}, f32[2,512,128]{2,1,0:T(8,128)}, f32[9,128,128]{2,1,0:T(8,128)}) custom-call(bf16[48,32,128]{2,1,0:T(8,128)(2,1)} %get-tuple-element.15.refs_0_, f32[4,8,8,512]{3,2,1,0:T(8,128)} %get-tuple-element.16.refs_1_, ...), custom_call_target="tpu_custom_call" | custom-call | tf_op jit(solution)/shard_map/pallas_call | solution.py:938

commit v3 on v2

--- a/solution.py
+++ b/solution.py
@@ -104,117 +104,117 @@
     lax.fori_loop(0, NB, one, 0)
 
 
+class Stream:
+    def __init__(self, src, pool, step, out_s, in_r):
+        self.src, self.pool, self.step = src, pool, step
+        self.out_s, self.in_r = out_s, in_r
+        self.bx, self.by = place()
+        self.mate = self.by + 1 - 2 * (self.by % 2)
+        if step:
+            self.kinds = [(6, None), (2, None), (0, None), (4, 0), (4, 1)]
+            self.sends = self.bx > 0 if step < 0 else self.bx < NX - 1
+            self.takes = self.bx < NX - 1 if step < 0 else self.bx > 0
+        else:
+            self.kinds = [(6, 0), (2, 1), (6, 1), (2, 0), (4, 0), (4, 1)]
+
+    def view(self, origin, half):
+        if half is None:
+            return self.pool.at[pl.ds(origin * NB, NB)]
+        return self.pool.at[pl.ds(origin * NB + half * (NB // 2), NB // 2)]
+
+    def when(self, ok, run):
+        if self.step:
+            pl.when(ok)(run)
+        else:
+            run()
+
+    def copy(self, src, origin, half, sem, kind, device):
+        got = self.in_r.at[7 if kind is None else self.kinds.index(kind)]
+        return remote(src, self.view(origin, half), self.out_s.at[sem], got, device)
+
+    def start(self):
+        def run():
+            for off, half in self.kinds:
+                if off == 4:
+                    continue
+                src = self.src if half is None else self.src.at[pl.ds(half * (NB // 2), NB // 2)]
+                to = (self.bx + self.step, (self.by + 8 - off) % NY)
+                self.copy(src, self.by, half, 0, (off, half), to).start()
+            if not self.step:
+                self.copy(self.src, self.by, None, 0, None, (self.bx, self.mate)).start()
+
+        self.when(self.sends if self.step else None, run)
+
+    def take(self, far):
+        def run():
+            for off, half in self.kinds:
+                if (off == 4) != far:
+                    continue
+                origin = (self.by + off) % NY
+                at = self.view(origin, half)
+                to_mate = self.copy(at, origin, half, 1, None, (self.bx, self.mate))
+                self.copy(at, origin, half, 1, (off, half), (self.bx, self.mate)).wait_recv()
+                part = 0 if off == 6 else 1
+                if off in (2, 6) and half in (None, part):
+                    piece = self.view(origin, part)
+                    to = (self.bx, (self.by + 8 - off) % NY)
+                    self.copy(piece, origin, part, 1, (4, part), to).start()
+                to_mate.start()
+
+        self.when(self.takes if self.step else None, run)
+
+    def bytes_of(self, messages, sem):
+        at = self.pool.at[pl.ds(0, messages * NB)]
+        return remote(at, at, self.out_s.at[sem], self.in_r.at[7], (self.bx, self.mate))
+
+    def finish(self):
+        self.when(self.takes if self.step else None, lambda: self.bytes_of(4, 1).wait_recv())
+
+    def drain(self):
+        self.when(self.sends if self.step else None, lambda: self.bytes_of(3, 0).wait_send())
+        passed = 5 if self.step else 4
+        self.when(self.takes if self.step else None, lambda: self.bytes_of(passed, 1).wait_send())
+
+
+STREAM_SEMS = [DMA((2,)), DMA((8,))]
+
+
 class Faces:
-    def __init__(self, msg, pool, side, own_s, fwd_s, side_s, sfwd_s, own_r, side_r):
+    def __init__(self, msg, pool, side, own, before, after):
         self.msg, self.pool, self.side = msg, pool, side
-        self.own_s, self.fwd_s, self.side_s, self.sfwd_s = own_s, fwd_s, side_s, sfwd_s
-        self.own_r, self.side_r = own_r, side_r
-        self.bx, self.by = place()
-        self.core = self.by % 2
-        self.mate = self.by + 1 - 2 * self.core
-
-    def first(self):
-        bx, by = self.bx, self.by
-        mine = pl.ds(by * NB, NB)
-        out = [
-            remote(self.msg, self.pool.at[mine], self.own_s.at[k], self.own_r.at[by], (bx, peer))
-            for k, peer in enumerate([self.mate] + [(by + 2 * k) % NY for k in (1, 2, 3)])
+        self.by = place()[1]
+        self.streams = [
+            Stream(msg, pool, 0, *own),
+            Stream(msg.at[:, 1], side.at[0], 1, *before),
+            Stream(msg.at[:, 0], side.at[1], -1, *after),
         ]
-        return out
-
-    def sides(self, to):
-        bx, by = self.bx, self.by
-        mine = pl.ds(by * NB, NB)
-        part, step = ((1, 1), (0, -1))[to]
-        return [
-            remote(
-                self.msg.at[:, part],
-                self.side.at[to, mine],
-                self.side_s.at[to, j],
-                self.side_r.at[to, by],
-                (bx + step, self.core + 2 * j),
-            )
-            for j in range(4)
-        ]
-
-    def has(self, to):
-        return (self.bx > 0, self.bx < NX - 1)[to]
-
-    def sends(self, to):
-        return self.has(1 - to)
 
     def start(self):
-        for c in self.first():
-            c.start()
-        for to in range(2):
-
-            @pl.when(self.sends(to))
-            def _(to=to):
-                for c in self.sides(to):
-                    c.start()
-
+        for x in self.streams:
+            x.start()
         self.pool[pl.ds(self.by * NB, NB)] = self.msg[...]
 
-    def own_landed(self, src, k):
-        at = self.pool.at[pl.ds(src * NB, NB)]
-        return remote(at, at, self.fwd_s.at[k], self.own_r.at[src], (self.bx, self.mate))
-
-    def side_landed(self, to, src, j):
-        at = self.side.at[to, pl.ds(src * NB, NB)]
-        return remote(at, at, self.sfwd_s.at[to, j], self.side_r.at[to, src], (self.bx, self.mate))
-
     def forward(self):
-        for k in (1, 3, 2):
-            c = self.own_landed((self.by + 2 * k) % NY, k - 1)
-            c.wait_recv()
-            c.start()
-        for to in range(2):
-
-            @pl.when(self.has(to))
-            def _(to=to):
-                for j in range(4):
-                    c = self.side_landed(to, self.core + 2 * j, j)
-                    c.wait_recv()
-                    c.start()
+        for far in (False, True):
+            for x in self.streams:
+                x.take(far)
 
     def finish(self):
-        for k in range(4):
-            self.own_landed((self.mate + 2 * k) % NY, 0).wait_recv()
-        for to in range(2):
-
-            @pl.when(self.has(to))
-            def _(to=to):
-                for j in range(4):
-                    self.side_landed(to, 1 - self.core + 2 * j, j).wait_recv()
+        for x in self.streams:
+            x.finish()
 
     def drain(self):
-        for c in self.first():
-            c.wait_send()
-        for k in (1, 2, 3):
-            self.own_landed((self.by + 2 * k) % NY, k - 1).wait_send()
-        for to in range(2):
-
-            @pl.when(self.sends(to))
-            def _(to=to):
-                for c in self.sides(to):
-                    c.wait_send()
-
-            @pl.when(self.has(to))
-            def _(to=to):
-                for j in range(4):
-                    self.side_landed(to, self.core + 2 * j, j).wait_send()
+        for x in self.streams:
+            x.drain()
 
 
 FACE_SCRATCH = [
     pltpu.VMEM((NB, 5, 32, 128), BF),
     pltpu.VMEM((GROUP + 1, 5, 32, 128), BF),
     pltpu.VMEM((2, GROUP + 1, 32, 128), BF),
-    DMA((4,)),
-    DMA((3,)),
-    DMA((2, 4)),
-    DMA((2, 4)),
-    DMA((NY,)),
-    DMA((2, NY)),
+    STREAM_SEMS,
+    STREAM_SEMS,
+    STREAM_SEMS,
 ]
 
 
@@ -379,56 +379,12 @@
     put(0, rim.row_in[0].astype(F32), corner[0][15:16], corner[1][0:1])
     put(ROWS + 1, rim.row_in[1].astype(F32), corner[2][15:16], corner[3][0:1])
 
-class Spread:
-    def __init__(self, src, pool, size, own_s, fwd_s, own_r):
-        self.src, self.pool, self.size = src, pool, size
-        self.own_s, self.fwd_s, self.own_r = own_s, fwd_s, own_r
-        self.bx, self.by = place()
-        self.mate = self.by + 1 - 2 * (self.by % 2)
-
-    def at(self, src):
-        return self.pool.at[pl.ds(src * self.size, self.size)]
-
-    def first(self):
-        peers = [(self.by + 2) % NY, (self.by + 6) % NY, (self.by + 4) % NY, self.mate]
-        return [
-            remote(self.src, self.at(self.by), self.own_s.at[k], self.own_r.at[self.by], (self.bx, peer))
-            for k, peer in enumerate(peers)
-        ]
-
-    def landed(self, src, k):
-        at = self.at(src)
-        return remote(at, at, self.fwd_s.at[k], self.own_r.at[src], (self.bx, self.mate))
-
-    def start(self):
-        for c in self.first():
-            c.start()
-        self.pool[pl.ds(self.by * self.size, self.size)] = self.src[...]
-
-    def forward(self):
-        for k in (1, 3, 2):
-            c = self.landed((self.by + 2 * k) % NY, k - 1)
-            c.wait_recv()
-            c.start()
-
-    def finish(self):
-        for k in range(4):
-            self.landed((self.mate + 2 * k) % NY, 0).wait_recv()
-
-    def drain(self):
-        for c in self.first():
-            c.wait_send()
-        for k in (1, 2, 3):
-            self.landed((self.by + 2 * k) % NY, k - 1).wait_send()
-
-
 class Total:
-    def __init__(self, base, half, cat, given, sums, second, ring, full, ms, mr, zs, zr, xs, xr, ws, wr, fs, fr):
+    def __init__(self, base, half, cat, given, sums, second, ring, full, sems):
         self.base, self.half, self.chunk = base, half, half // NX
         self.cat, self.given, self.sums, self.second = cat, given, sums, second
         self.ring, self.full = ring, full
-        self.ms, self.mr, self.zs, self.zr, self.xs, self.xr = ms, mr, zs, zr, xs, xr
-        self.ws, self.wr, self.fs, self.fr = ws, wr, fs, fr
+        self.sems = sems
         self.bx, self.by = place()
         self.core = self.by % 2
         self.mate = self.by + 1 - 2 * self.core
@@ -442,11 +398,10 @@
 
     def to_mate(self):
         at = self.cat.at[self.rows(1 - self.core)]
-        return remote(at, self.given, self.ms.at[0], self.mr.at[0], (self.bx, self.mate))
-
-    def to_x(self, q):
-        at = self.sums.at[pl.ds(q * self.chunk, self.chunk)]
-        return remote(at, self.second.at[self.bx], self.zs.at[q], self.zr.at[self.bx], (q, self.by))
+        return remote(at, self.given, self.sems.at[0], self.sems.at[1], (self.bx, self.mate))
+
+    def all_of(self, at, stage):
+        return remote(at, at, self.sems.at[2 * stage], self.sems.at[2 * stage + 1], (self.bx, self.mate))
 
     def combine(self):
         self.to_mate().wait_recv()
@@ -455,72 +410,48 @@
 
             @pl.when(self.bx != q)
             def _(q=q):
-                self.to_x(q).start()
-
-    def to_ring(self, k):
-        at = self.ring.at[self.chip]
-        to = (self.by + 2 * k) % NY
-        return remote(at, at, self.xs.at[k], self.xr.at[self.chip], (self.bx, to))
+                at = self.sums.at[pl.ds(q * self.chunk, self.chunk)]
+                remote(at, self.second.at[self.bx], self.sems.at[2], self.sems.at[3], (q, self.by)).start()
 
     def sum_x(self):
+        self.all_of(self.second.at[pl.ds(0, NX - 1)], 1).wait_recv()
         mine = pl.ds(pl.multiple_of(self.bx * self.chunk, self.chunk), self.chunk)
         total = self.sums[mine].astype(F32)
         for k in range(1, NX):
-            src = (self.bx + k) % NX
-            at = self.second.at[src]
-            remote(at, at, self.zs.at[0], self.zr.at[src], (src, self.by)).wait_recv()
-            total = total + self.second[src].astype(F32)
+            total = total + self.second[(self.bx + k) % NX].astype(F32)
         self.ring[self.chip] = total.astype(BF)
+        at = self.ring.at[self.chip]
         for k in (1, 3, 2):
-            self.to_ring(k).start()
-
-    def out_x(self, k):
-        at = self.full.at[self.piece(self.core, self.bx)]
-        return remote(at, at, self.ws.at[k], self.wr.at[self.bx], ((self.bx + k) % NX, self.by))
-
-    def pass_on(self, src):
-        at = self.full.at[self.piece(self.core, src)]
-        return remote(at, at, self.fs.at[src], self.fr.at[src], (self.bx, self.mate))
+            to = (self.bx, (self.by + 2 * k) % NY)
+            remote(at, at, self.sems.at[4], self.sems.at[5], to).start()
 
     def sum_ring(self):
-        for k in range(1, 4):
-            src = (self.chip + k) % 4
-            at = self.ring.at[src]
-            remote(at, at, self.xs.at[k], self.xr.at[src], (self.bx, src * 2 + self.core)).wait_recv()
+        self.all_of(self.ring.at[pl.ds(0, 3)], 2).wait_recv()
         total = self.ring[0].astype(F32)
         for i in range(1, 4):
             total = total + self.ring[i].astype(F32)
         self.full[self.piece(self.core, self.bx)] = total.astype(BF)
+        at = self.full.at[self.piece(self.core, self.bx)]
         for k in range(1, NX):
-            self.out_x(k).start()
-        self.pass_on(self.bx).start()
+            remote(at, at, self.sems.at[6], self.sems.at[7], ((self.bx + k) % NX, self.by)).start()
+
+    def share(self):
+        at = self.full.at[pl.ds(pl.multiple_of(self.core * self.half, self.half), self.half)]
+        return remote(at, at, self.sems.at[8], self.sems.at[9], (self.bx, self.mate))
 
     def relay(self):
-        for k in range(1, NX):
-            src = (self.bx + k) % NX
-            at = self.full.at[self.piece(self.core, src)]
-            remote(at, at, self.ws.at[k], self.wr.at[src], (src, self.by)).wait_recv()
-            self.pass_on(src).start()
+        self.all_of(self.full.at[pl.ds(0, (NX - 1) * self.chunk)], 3).wait_recv()
+        self.share().start()
 
     def done(self):
-        for src in range(NX):
-            at = self.full.at[self.piece(1 - self.core, src)]
-            remote(at, at, self.fs.at[src], self.fr.at[src], (self.bx, self.mate)).wait_recv()
+        self.share().wait_recv()
 
     def drain(self):
         self.to_mate().wait_send()
-        for q in range(NX):
-
-            @pl.when(self.bx != q)
-            def _(q=q):
-                self.to_x(q).wait_send()
-
-        for k in range(1, 4):
-            self.to_ring(k).wait_send()
-        for k in range(1, NX):
-            self.out_x(k).wait_send()
-        for src in range(NX):
-            self.pass_on(src).wait_send()
+        self.all_of(self.second.at[pl.ds(0, NX - 1)], 1).wait_send()
+        self.all_of(self.ring.at[pl.ds(0, 3)], 2).wait_send()
+        self.all_of(self.full.at[pl.ds(0, (NX - 1) * self.chunk)], 3).wait_send()
+        self.share().wait_send()
 
 
 def total_scratch(half):
@@ -531,7 +462,7 @@
         pltpu.VMEM((NX, chunk, 128), BF),
         pltpu.VMEM((4, chunk, 128), BF),
         pltpu.VMEM((2 * half, 128), BF),
-        *[DMA((n,)) for n in (1, 1, NX, NX, 4, 4, NX, NX, NX, NX)],
+        DMA((10,)),
     ]
 
 
@@ -592,7 +523,7 @@
     pack_faces(cur, faces.msg, coords)
     met()
     tell = [
-        remote(code, codes_v.at[by], code_s.at[k], code_r.at[by], (bx, (by + k) % NY)) for k in range(1, NY)
+        remote(code, codes_v.at[by], code_s.at[0], code_r.at[0], (bx, (by + k) % NY)) for k in range(1, NY)
     ]
     for c in tell:
         c.start()
@@ -618,9 +549,9 @@
         return carry
 
     lax.fori_loop(0, 9, build, 0)
-    for k in range(1, NY):
-        src = (by + k) % NY
-        remote(code, codes_v.at[src], code_s.at[k], code_r.at[src], (bx, src)).wait_recv()
+    others = codes_v.at[pl.ds(0, NY - 1)]
+    told = remote(others, others, code_s.at[0], code_r.at[0], (bx, (by + 1) % NY))
+    told.wait_recv()
     to_scalar = pltpu.make_async_copy(codes_v.at[:, 0], codes, code_l.at[0])
     to_scalar.start()
     to_scalar.wait()
@@ -654,11 +585,13 @@
         high = coords[2, n].astype(F32)
         one = fold_both[:, n, :, 0:128] * (1.0 - high) + fold_both[:, n, :, 128:256] * high
         part[n] = one.reshape(64, 128).astype(BF)
-    parts = Spread(part, part_pool, NB, *part_sems)
+    parts = Stream(part, part_pool, 0, *part_sems)
     parts.start()
+    part_pool[pl.ds(by * NB, NB)] = part[...]
     loads[3].wait()
     loads[4].wait()
-    parts.forward()
+    parts.take(False)
+    parts.take(True)
     parts.finish()
 
     rims = [
@@ -735,8 +668,8 @@
         remote(
             ready.at[pl.ds((by + k) % NY * NB, NB)],
             back.at[by],
-            back_s.at[k],
-            back_r.at[by],
+            back_s.at[0],
+            back_r.at[0],
             (bx, (by + k) % NY),
         )
         for k in (4, 3, 5, 2, 6, 1, 7)
@@ -745,9 +678,9 @@
         c.start()
     back[by] = ready[pl.ds(by * NB, NB)]
     pl.when(core == 0)(early.combine)
-    for k in range(1, NY):
-        src = (by + k) % NY
-        remote(ready.at[pl.ds(0, NB)], back.at[src], back_s.at[k], back_r.at[src], (bx, src)).wait_recv()
+    others = back.at[pl.ds(0, NY - 1)]
+    came = remote(others, others, back_s.at[0], back_r.at[0], (bx, (by + 1) % NY))
+    came.wait_recv()
 
     for n in range(NB):
         high = coords[2, n].astype(F32)
@@ -826,8 +759,8 @@
         conv_out[t, 96:192] = v[:, 64:128]
     stores[2].start()
 
-    for c in tell + give:
-        c.wait_send()
+    told.wait_send()
+    came.wait_send()
     faces.drain()
     back_faces.drain()
     parts.drain()
@@ -906,9 +839,9 @@
             total_scratch(512),
             FACE_SCRATCH,
             FACE_SCRATCH,
-            [DMA((4,)), DMA((3,)), DMA((NY,))],
-            DMA((NY,)),
-            DMA((NY,)),
+            STREAM_SEMS,
+            DMA((1,)),
+            DMA((1,)),
             DMA((1,)),
             pltpu.VMEM((2, 2, COLS, 128), BF),
             pltpu.VMEM((2, 2, ROWS, 128), BF),
@@ -917,8 +850,8 @@
             pltpu.VMEM((2, 4, 16, 128), BF),
             DMA((2, 8)),
             DMA((2, 8)),
-            DMA((NY,)),
-            DMA((NY,)),
+            DMA((1,)),
+            DMA((1,)),
         ],
         compiler_params=pltpu.CompilerParams(
             collective_id=1, has_side_effects=True, vmem_limit_bytes=58 * 2**20

time: 85.7 us -> 82 us (0.957)
  Pallas kernels: 84.9 us -> 81.2 us
    pallas_call x1, Pallas kernels: 82 us -> 78.4 us  [body(): pl.pallas_call(whole, in_specs=[far] * 5 + [VMEM] * 3 + [SMEM] * 2, out_s...]
where the time goes in v3:
time: 82 us; the launch traced here: 81.8 us
  Pallas kernels  81.2 us (99%)
    pallas_call x1, Pallas kernels, body(): pl.pallas_call(whole, in_specs=[far] * 5 + [VMEM] * 3 + [SMEM] * 2, out_s...  78.4 us
    pallas_call x1, Pallas kernels, body(): pl.pallas_call(hand_on, in_specs=[far] * 5, out_specs=[far] * 5, out_shap...  2.82 us

profile of v3, /device:TPU:1, one launch (start us, length us, event | category | flops | bytes accessed | tf_op | source)
XLA Modules:
  0.0 81.8 jit_solution(6294289541742085012)
XLA Ops:
  0.6 78.4 %shard_map.137 = (bf16[48,32,128]{2,1,0:T(8,128)(2,1)}, f32[4,8,8,512]{3,2,1,0:T(8,128)}, f32[9,192,64]{2,1,0:T(8,128)}, f32[2,512,128]{2,1,0:T(8,128)}, f32[9,128,128]{2,1,0:T(8,128)}) custom-call(bf16[4,8,8,512]{3,2,1,0:T(8,128)(2,1)} %vox_h.1, bf16[27,64,64]{2,1,0:T(8,128)(2,1)} %bitcast.10, bf16[2,512,128]{2,1,0:T(8,128)(2,1)} %bitcast.12, ...), custom_call_target="tpu_custom_call" | custom-call | tf_op jit(solution)/shard_map/pallas_call | solution.py:797
  79.0 2.8 %shard_map.138 = (bf16[48,32,128]{2,1,0:T(8,128)(2,1)}, f32[4,8,8,512]{3,2,1,0:T(8,128)}, f32[9,192,64]{2,1,0:T(8,128)}, f32[2,512,128]{2,1,0:T(8,128)}, f32[9,128,128]{2,1,0:T(8,128)}) custom-call(bf16[48,32,128]{2,1,0:T(8,128)(2,1)} %get-tuple-element.15.refs_0_, f32[4,8,8,512]{3,2,1,0:T(8,128)} %get-tuple-element.16.refs_1_, ...), custom_call_target="tpu_custom_call" | custom-call | tf_op jit(solution)/shard_map/pallas_call | solution.py:871

commit v4 on v3

--- a/solution.py
+++ b/solution.py
@@ -101,12 +101,12 @@
         msg[n, 4] = jnp.where(lane < 64, face[0:32], pltpu.roll(face[32:64], 64, 1)).astype(BF)
         return carry
 
-    lax.fori_loop(0, NB, one, 0)
+    lax.fori_loop(0, NB, one, 0, unroll=True)
 
 
 class Stream:
-    def __init__(self, src, pool, step, out_s, in_r):
-        self.src, self.pool, self.step = src, pool, step
+    def __init__(self, src, pool, step, out_s, in_r, straight=False):
+        self.src, self.pool, self.step, self.straight = src, pool, step, straight
         self.out_s, self.in_r = out_s, in_r
         self.bx, self.by = place()
         self.mate = self.by + 1 - 2 * (self.by % 2)
@@ -114,6 +114,8 @@
             self.kinds = [(6, None), (2, None), (0, None), (4, 0), (4, 1)]
             self.sends = self.bx > 0 if step < 0 else self.bx < NX - 1
             self.takes = self.bx < NX - 1 if step < 0 else self.bx > 0
+        elif straight:
+            self.kinds = [(4, None), (6, None), (2, None)]
         else:
             self.kinds = [(6, 0), (2, 1), (6, 1), (2, 0), (4, 0), (4, 1)]
 
@@ -135,7 +137,7 @@
     def start(self):
         def run():
             for off, half in self.kinds:
-                if off == 4:
+                if off == 4 and not self.straight:
                     continue
                 src = self.src if half is None else self.src.at[pl.ds(half * (NB // 2), NB // 2)]
                 to = (self.bx + self.step, (self.by + 8 - off) % NY)
@@ -147,7 +149,7 @@
 
     def take(self, far):
         def run():
-            for off, half in self.kinds:
+            for off, half in reversed(self.kinds) if self.straight else self.kinds:
                 if (off == 4) != far:
                     continue
                 origin = (self.by + off) % NY
@@ -155,7 +157,7 @@
                 to_mate = self.copy(at, origin, half, 1, None, (self.bx, self.mate))
                 self.copy(at, origin, half, 1, (off, half), (self.bx, self.mate)).wait_recv()
                 part = 0 if off == 6 else 1
-                if off in (2, 6) and half in (None, part):
+                if off in (2, 6) and half in (None, part) and not self.straight:
                     piece = self.view(origin, part)
                     to = (self.bx, (self.by + 8 - off) % NY)
                     self.copy(piece, origin, part, 1, (4, part), to).start()
@@ -171,8 +173,8 @@
         self.when(self.takes if self.step else None, lambda: self.bytes_of(4, 1).wait_recv())
 
     def drain(self):
-        self.when(self.sends if self.step else None, lambda: self.bytes_of(3, 0).wait_send())
-        passed = 5 if self.step else 4
+        self.when(self.sends if self.step else None, lambda: self.bytes_of(4 if self.straight else 3, 0).wait_send())
+        passed = 5 if self.step else 3 if self.straight else 4
         self.when(self.takes if self.step else None, lambda: self.bytes_of(passed, 1).wait_send())
 
 
@@ -284,7 +286,7 @@
                 put(x + 1, t, z[t], edge[0, x : x + 1, lanes], edge[1, x : x + 1, lanes])
         return carry
 
-    lax.fori_loop(0, NB, one, 0)
+    lax.fori_loop(0, NB, one, 0, unroll=2)
 
 
 NEAR = [(-1, 0), (1, 0), (0, -1), (0, 1), (-1, -1), (-1, 1), (1, -1), (1, 1)]
@@ -374,7 +376,7 @@
         put(i + 1, plane[i], side32[0, pl.ds(i, 1), :], side32[1, pl.ds(i, 1), :])
         return carry
 
-    lax.fori_loop(0, ROWS, inner, 0)
+    lax.fori_loop(0, ROWS, inner, 0, unroll=8)
     corner = [rim.corner_in[c].astype(F32) for c in range(4)]
     put(0, rim.row_in[0].astype(F32), corner[0][15:16], corner[1][0:1])
     put(ROWS + 1, rim.row_in[1].astype(F32), corner[2][15:16], corner[3][0:1])
@@ -585,7 +587,7 @@
         high = coords[2, n].astype(F32)
         one = fold_both[:, n, :, 0:128] * (1.0 - high) + fold_both[:, n, :, 128:256] * high
         part[n] = one.reshape(64, 128).astype(BF)
-    parts = Stream(part, part_pool, 0, *part_sems)
+    parts = Stream(part, part_pool, 0, *part_sems, straight=True)
     parts.start()
     part_pool[pl.ds(by * NB, NB)] = part[...]
     loads[3].wait()
@@ -622,7 +624,7 @@
         gplane[pl.ds(i * BS, BS)] = rounded(g).reshape(BS, COLS, 128)
         return carry
 
-    lax.fori_loop(0, TR, ahead, 0)
+    lax.fori_loop(0, TR, ahead, 0, unroll=3)
     stores[0].start()
     rims[1].start(gplane)
     turned = gplane[...].reshape(ROWS * COLS, 128).T.astype(BF)
@@ -654,7 +656,7 @@
             slots[i * TC + c] = grad[:, c * BS : (c + 1) * BS, :].reshape(64, 128).astype(BF)
         return carry
 
-    lax.fori_loop(0, TR, behind, 0)
+    lax.fori_loop(0, TR, behind, 0, unroll=3)
 
     def fill(b, carry):
         number = codes[b // NB, b % NB] // 2
@@ -663,7 +665,7 @@
         ready[b] = slots[jnp.clip(at, 0, TR * TC - 1)]
         return carry
 
-    lax.fori_loop(0, GROUP, fill, 0)
+    lax.fori_loop(0, GROUP, fill, 0, unroll=8)
     give = [
         remote(
             ready.at[pl.ds((by + k) % NY * NB, NB)],
@@ -724,9 +726,12 @@
     pl.when(core == 1)(early.combine)
     late.combine()
     early.sum_x()
+    for x in back_faces.streams:
+        x.take(False)
     late.sum_x()
     early.sum_ring()
-    back_faces.forward()
+    for x in back_faces.streams:
+        x.take(True)
     late.sum_ring()
     back_faces.finish()
     assemble(cur, back_faces.pool, back_faces.side, neighbors, shifted, edge)

time: 82 us -> 76.1 us (0.928)
  Pallas kernels: 81.2 us -> 75.2 us
    pallas_call x1, Pallas kernels: 78.4 us -> 72.4 us  [body(): pl.pallas_call(whole, in_specs=[far] * 5 + [VMEM] * 3 + [SMEM] * 2, out_s...]
where the time goes in v4:
time: 76.1 us; the launch traced here: 75.9 us
  Pallas kernels  75.2 us (99%)
    pallas_call x1, Pallas kernels, body(): pl.pallas_call(whole, in_specs=[far] * 5 + [VMEM] * 3 + [SMEM] * 2, out_s...  72.4 us
    pallas_call x1, Pallas kernels, body(): pl.pallas_call(hand_on, in_specs=[far] * 5, out_specs=[far] * 5, out_shap...  2.82 us

profile of v4, /device:TPU:1, one launch (start us, length us, event | category | flops | bytes accessed | tf_op | source)
XLA Modules:
  0.0 75.9 jit_solution(8540769921472819752)
XLA Ops:
  0.6 72.4 %shard_map.137 = (bf16[48,32,128]{2,1,0:T(8,128)(2,1)}, f32[4,8,8,512]{3,2,1,0:T(8,128)}, f32[9,192,64]{2,1,0:T(8,128)}, f32[2,512,128]{2,1,0:T(8,128)}, f32[9,128,128]{2,1,0:T(8,128)}) custom-call(bf16[4,8,8,512]{3,2,1,0:T(8,128)(2,1)} %vox_h.1, bf16[27,64,64]{2,1,0:T(8,128)(2,1)} %bitcast.10, bf16[2,512,128]{2,1,0:T(8,128)(2,1)} %bitcast.12, ...), custom_call_target="tpu_custom_call" | custom-call | tf_op jit(solution)/shard_map/pallas_call | solution.py:802
  73.1 2.8 %shard_map.138 = (bf16[48,32,128]{2,1,0:T(8,128)(2,1)}, f32[4,8,8,512]{3,2,1,0:T(8,128)}, f32[9,192,64]{2,1,0:T(8,128)}, f32[2,512,128]{2,1,0:T(8,128)}, f32[9,128,128]{2,1,0:T(8,128)}) custom-call(bf16[48,32,128]{2,1,0:T(8,128)(2,1)} %get-tuple-element.15.refs_0_, f32[4,8,8,512]{3,2,1,0:T(8,128)} %get-tuple-element.16.refs_1_, ...), custom_call_target="tpu_custom_call" | custom-call | tf_op jit(solution)/shard_map/pallas_call | solution.py:876

commit v5 on v4

--- a/solution.py
+++ b/solution.py
@@ -286,7 +286,7 @@
                 put(x + 1, t, z[t], edge[0, x : x + 1, lanes], edge[1, x : x + 1, lanes])
         return carry
 
-    lax.fori_loop(0, NB, one, 0, unroll=2)
+    lax.fori_loop(0, NB, one, 0, unroll=True)
 
 
 NEAR = [(-1, 0), (1, 0), (0, -1), (0, 1), (-1, -1), (-1, 1), (1, -1), (1, 1)]
@@ -376,7 +376,7 @@
         put(i + 1, plane[i], side32[0, pl.ds(i, 1), :], side32[1, pl.ds(i, 1), :])
         return carry
 
-    lax.fori_loop(0, ROWS, inner, 0, unroll=8)
+    lax.fori_loop(0, ROWS, inner, 0, unroll=16)
     corner = [rim.corner_in[c].astype(F32) for c in range(4)]
     put(0, rim.row_in[0].astype(F32), corner[0][15:16], corner[1][0:1])
     put(ROWS + 1, rim.row_in[1].astype(F32), corner[2][15:16], corner[3][0:1])
@@ -482,8 +482,8 @@
 
 def whole(
     vox_h, conv_w_h, fold_w_h, map_w_h, cot_h, conv_b, fold_b, map_b, coords, neighbors,
-    bev_far, feat_far, conv_far, fold_far, map_far,
-    bev_out, feat_out, conv_out, fold_out, map_out, out_sem,
+    bev_far, feat_far, early_far, late_far,
+    bev_out, feat_out, out_sem,
     vox, conv_w, fold_w, map_w, cot, load_sem,
     cur, shifted, edge, toep, toep_back, wide, pre, act, fold_both, part, part_pool,
     code, codes_v, codes, table,
@@ -497,7 +497,12 @@
     stores = [
         pltpu.make_async_copy(src, dst, out_sem.at[i])
         for i, (src, dst) in enumerate(
-            ((bev_out, bev_far), (feat_out, feat_far), (conv_out, conv_far), (fold_out, fold_far), (map_out, map_far))
+            (
+                (bev_out, bev_far),
+                (feat_out, feat_far),
+                (early_part[4], early_far),
+                (late_part[4], late_far),
+            )
         )
     ]
     early = Total(0, 1024, cat, *early_part)
@@ -568,6 +573,7 @@
 
     lax.fori_loop(0, TR * TC * 2, look, 0)
     faces.forward()
+    loads[3].wait()
     faces.finish()
     assemble(cur, faces.pool, faces.side, neighbors, shifted, edge)
     for e in range(3):
@@ -590,11 +596,20 @@
     parts = Stream(part, part_pool, 0, *part_sems, straight=True)
     parts.start()
     part_pool[pl.ds(by * NB, NB)] = part[...]
-    loads[3].wait()
     loads[4].wait()
     parts.take(False)
     parts.take(True)
     parts.finish()
+
+    def fill_slot(r, c):
+        total = fold_b[...]
+        for h in range(2):
+            at = table[(r * TC + c) * 2 + h]
+            here = (at < GROUP).astype(F32)
+            total = total + part_pool[jnp.minimum(at, GROUP - 1)].astype(F32) * here
+        where = (slice(r * BS, (r + 1) * BS), slice(c * BS, (c + 1) * BS))
+        fold[where] = total.reshape(BS, BS, 128)
+        plane[where] = rounded(total * jax.nn.sigmoid(total)).reshape(BS, BS, 128)
 
     rims = [
         Rim(row_out.at[p], col_out.at[p], row_in.at[p], col_in.at[p], corner_in.at[p], rim_s.at[p], rim_r.at[p])
@@ -602,14 +617,7 @@
     ]
     for r in range(TR):
         for c in range(TC):
-            total = fold_b[...]
-            for h in range(2):
-                at = table[(r * TC + c) * 2 + h]
-                here = (at < GROUP).astype(F32)
-                total = total + part_pool[jnp.minimum(at, GROUP - 1)].astype(F32) * here
-            where = (slice(r * BS, (r + 1) * BS), slice(c * BS, (c + 1) * BS))
-            fold[where] = total.reshape(BS, BS, 128)
-            plane[where] = rounded(total * jax.nn.sigmoid(total)).reshape(BS, BS, 128)
+            fill_slot(r, c)
     rims[0].start(plane)
     rims[0].finish()
     spread(plane, rims[0], side32, spread_mid)
@@ -624,7 +632,7 @@
         gplane[pl.ds(i * BS, BS)] = rounded(g).reshape(BS, COLS, 128)
         return carry
 
-    lax.fori_loop(0, TR, ahead, 0, unroll=3)
+    lax.fori_loop(0, TR, ahead, 0, unroll=True)
     stores[0].start()
     rims[1].start(gplane)
     turned = gplane[...].reshape(ROWS * COLS, 128).T.astype(BF)
@@ -656,7 +664,7 @@
             slots[i * TC + c] = grad[:, c * BS : (c + 1) * BS, :].reshape(64, 128).astype(BF)
         return carry
 
-    lax.fori_loop(0, TR, behind, 0, unroll=3)
+    lax.fori_loop(0, TR, behind, 0, unroll=True)
 
     def fill(b, carry):
         number = codes[b // NB, b % NB] // 2
@@ -665,7 +673,7 @@
         ready[b] = slots[jnp.clip(at, 0, TR * TC - 1)]
         return carry
 
-    lax.fori_loop(0, GROUP, fill, 0, unroll=8)
+    lax.fori_loop(0, GROUP, fill, 0, unroll=True)
     give = [
         remote(
             ready.at[pl.ds((by + k) % NY * NB, NB)],
@@ -750,19 +758,9 @@
     early.relay()
     late.relay()
     early.done()
-    for h in range(2):
-        fold_out[h] = early.full[1024 + h * 512 : 1024 + (h + 1) * 512].astype(F32)
+    stores[2].start()
+    late.done()
     stores[3].start()
-    for t in range(8):
-        map_out[t] = early.full[t * 128 : (t + 1) * 128].astype(F32)
-    late.done()
-    map_out[8] = late.full[0:128].astype(F32)
-    stores[4].start()
-    for t in range(9):
-        v = late.full[128 + t * 96 : 128 + (t + 1) * 96].astype(F32)
-        conv_out[t, 0:96] = v[:, 0:64]
-        conv_out[t, 96:192] = v[:, 64:128]
-    stores[2].start()
 
     told.wait_send()
     came.wait_send()
@@ -777,15 +775,40 @@
         c.wait()
 
 
-def hand_on(*refs):
-    given, results, held, sems = refs[:5], refs[5:10], refs[10:15], refs[15]
-    takes = [pltpu.make_async_copy(a, b, sems.at[0, i]) for i, (a, b) in enumerate(zip(given, held, strict=True))]
-    gives = [pltpu.make_async_copy(a, b, sems.at[1, i]) for i, (a, b) in enumerate(zip(held, results, strict=True))]
+def hand_on(
+    bev_in, feat_in, early_in, late_in, bev_far, feat_far, conv_far, fold_far, map_far,
+    bev, feat, early, late, conv, fold, grads, sems,
+):
+    takes = [
+        pltpu.make_async_copy(a, b, sems.at[0, i])
+        for i, (a, b) in enumerate(((early_in, early), (late_in, late), (bev_in, bev), (feat_in, feat)))
+    ]
     for c in takes:
         c.start()
-    for take, give in zip(takes, gives, strict=True):
-        take.wait()
-        give.start()
+    gives = [
+        pltpu.make_async_copy(a, b, sems.at[1, i])
+        for i, (a, b) in enumerate(
+            ((grads, map_far), (fold, fold_far), (conv, conv_far), (bev, bev_far), (feat, feat_far))
+        )
+    ]
+    takes[2].wait()
+    gives[3].start()
+    takes[3].wait()
+    gives[4].start()
+    takes[0].wait()
+    for h in range(2):
+        fold[h] = early[1024 + h * 512 : 1024 + (h + 1) * 512].astype(F32)
+    gives[1].start()
+    for t in range(8):
+        grads[t] = early[t * 128 : (t + 1) * 128].astype(F32)
+    takes[1].wait()
+    grads[8] = late[0:128].astype(F32)
+    gives[0].start()
+    for t in range(9):
+        v = late[128 + t * 96 : 128 + (t + 1) * 96].astype(F32)
+        conv[t, 0:96] = v[:, 0:64]
+        conv[t, 96:192] = v[:, 64:128]
+    gives[2].start()
     for c in gives:
         c.wait()
 
@@ -799,14 +822,15 @@
         jax.ShapeDtypeStruct((2, 512, 128), F32),
         jax.ShapeDtypeStruct((9, 128, 128), F32),
     ]
+    between = outs[:2] + [jax.ShapeDtypeStruct((2048, 128), BF), jax.ShapeDtypeStruct((1024, 128), BF)]
     made = pl.pallas_call(
         whole,
         in_specs=[far] * 5 + [VMEM] * 3 + [SMEM] * 2,
-        out_specs=[far] * 5,
-        out_shape=outs,
+        out_specs=[far] * 4,
+        out_shape=between,
         scratch_shapes=[
-            *[pltpu.VMEM(o.shape, o.dtype) for o in outs],
-            DMA((5,)),
+            *[pltpu.VMEM(o.shape, o.dtype) for o in outs[:2]],
+            DMA((4,)),
             pltpu.VMEM((NB, BS, BS, 512), BF),
             pltpu.VMEM((27, 64, 64), BF),
             pltpu.VMEM((2, 512, 128), BF),
@@ -875,10 +899,10 @@
     )
     bev_map, feat_grad, conv_grads, fold_grads, map_grads = pl.pallas_call(
         hand_on,
-        in_specs=[far] * 5,
+        in_specs=[far] * 4,
         out_specs=[far] * 5,
         out_shape=outs,
-        scratch_shapes=[*[pltpu.VMEM(o.shape, o.dtype) for o in outs], DMA((2, 5))],
+        scratch_shapes=[*[pltpu.VMEM(o.shape, o.dtype) for o in between + outs[2:]], DMA((2, 5))],
         compiler_params=pltpu.CompilerParams(vmem_limit_bytes=58 * 2**20),
     )(*made)
     return (

time: 76.1 us -> 74.6 us (0.980)
  Pallas kernels: 75.2 us -> 73.7 us
    pallas_call x1, Pallas kernels: 72.4 us -> 70.8 us  [body(): pl.pallas_call(whole, in_specs=[far] * 5 + [VMEM] * 3 + [SMEM] * 2, out_s...]
where the time goes in v5:
time: 74.6 us; the launch traced here: 74.4 us
  Pallas kernels  73.7 us (99%)
    pallas_call x1, Pallas kernels, body(): pl.pallas_call(whole, in_specs=[far] * 5 + [VMEM] * 3 + [SMEM] * 2, out_s...  70.8 us
    pallas_call x1, Pallas kernels, body(): pl.pallas_call(hand_on, in_specs=[far] * 4, out_specs=[far] * 5, out_shap...  2.94 us

profile of v5, /device:TPU:1, one launch (start us, length us, event | category | flops | bytes accessed | tf_op | source)
XLA Modules:
  0.0 74.4 jit_solution(8915042475729235973)
XLA Ops:
  0.6 70.8 %shard_map.137 = (bf16[48,32,128]{2,1,0:T(8,128)(2,1)}, f32[4,8,8,512]{3,2,1,0:T(8,128)}, bf16[2048,128]{1,0:T(8,128)(2,1)}, bf16[1024,128]{1,0:T(8,128)(2,1)}) custom-call(bf16[4,8,8,512]{3,2,1,0:T(8,128)(2,1)} %vox_h.1, bf16[27,64,64]{2,1,0:T(8,128)(2,1)} %bitcast.10, bf16[2,512,128]{2,1,0:T(8,128)(2,1)} %bitcast.12, bf16[3,384,128]{2,1,0:T(8,128)(2,1)} %bitcast.11, ...), custom_call_target="tpu_custom_call" | custom-call | tf_op jit(solution)/shard_map/pallas_call | solution.py:826
  71.4 2.9 %shard_map.138 = (bf16[48,32,128]{2,1,0:T(8,128)(2,1)}, f32[4,8,8,512]{3,2,1,0:T(8,128)}, f32[9,192,64]{2,1,0:T(8,128)}, f32[2,512,128]{2,1,0:T(8,128)}, f32[9,128,128]{2,1,0:T(8,128)}) custom-call(bf16[48,32,128]{2,1,0:T(8,128)(2,1)} %get-tuple-element.14.bev_in, f32[4,8,8,512]{3,2,1,0:T(8,128)} %get-tuple-element.15.feat_in, ...), custom_call_target="tpu_custom_call" | custom-call | tf_op jit(solution)/shard_map/pallas_call | solution.py:900

commit v6 on v5

--- a/solution.py
+++ b/solution.py
@@ -743,6 +743,7 @@
     late.sum_ring()
     back_faces.finish()
     assemble(cur, back_faces.pool, back_faces.side, neighbors, shifted, edge)
+    early.relay()
     for e in range(3):
         wide[:, e * 640 : (e + 1) * 640] = shifted[e].astype(BF)
     for g in range(4):
@@ -755,7 +756,6 @@
         for n in range(NB):
             feat_out[n, :, :, g * 128 : (g + 1) * 128] = view[:, n]
     stores[1].start()
-    early.relay()
     late.relay()
     early.done()
     stores[2].start()
@@ -781,7 +781,7 @@
 ):
     takes = [
         pltpu.make_async_copy(a, b, sems.at[0, i])
-        for i, (a, b) in enumerate(((early_in, early), (late_in, late), (bev_in, bev), (feat_in, feat)))
+        for i, (a, b) in enumerate(((feat_in, feat), (bev_in, bev), (early_in, early), (late_in, late)))
     ]
     for c in takes:
         c.start()
@@ -791,17 +791,17 @@
             ((grads, map_far), (fold, fold_far), (conv, conv_far), (bev, bev_far), (feat, feat_far))
         )
     ]
+    takes[0].wait()
+    gives[4].start()
+    takes[1].wait()
+    gives[3].start()
     takes[2].wait()
-    gives[3].start()
-    takes[3].wait()
-    gives[4].start()
-    takes[0].wait()
     for h in range(2):
         fold[h] = early[1024 + h * 512 : 1024 + (h + 1) * 512].astype(F32)
     gives[1].start()
     for t in range(8):
         grads[t] = early[t * 128 : (t + 1) * 128].astype(F32)
-    takes[1].wait()
+    takes[3].wait()
     grads[8] = late[0:128].astype(F32)
     gives[0].start()
     for t in range(9):

time: 74.6 us -> 74.4 us (level)
  no operation moved by 1% of the time
where the time goes in v6:
time: 74.4 us; the launch traced here: 74.2 us
  Pallas kernels  73.5 us (99%)
    pallas_call x1, Pallas kernels, body(): pl.pallas_call(whole, in_specs=[far] * 5 + [VMEM] * 3 + [SMEM] * 2, out_s...  70.8 us
    pallas_call x1, Pallas kernels, body(): pl.pallas_call(hand_on, in_specs=[far] * 4, out_specs=[far] * 5, out_shap...  2.72 us

profile of v6, /device:TPU:1, one launch (start us, length us, event | category | flops | bytes accessed | tf_op | source)
XLA Modules:
  0.0 74.2 jit_solution(3448710172969413903)
XLA Ops:
  0.6 70.8 %shard_map.137 = (bf16[48,32,128]{2,1,0:T(8,128)(2,1)}, f32[4,8,8,512]{3,2,1,0:T(8,128)}, bf16[2048,128]{1,0:T(8,128)(2,1)}, bf16[1024,128]{1,0:T(8,128)(2,1)}) custom-call(bf16[4,8,8,512]{3,2,1,0:T(8,128)(2,1)} %vox_h.1, bf16[27,64,64]{2,1,0:T(8,128)(2,1)} %bitcast.10, bf16[2,512,128]{2,1,0:T(8,128)(2,1)} %bitcast.12, bf16[3,384,128]{2,1,0:T(8,128)(2,1)} %bitcast.11, ...), custom_call_target="tpu_custom_call" | custom-call | tf_op jit(solution)/shard_map/pallas_call | solution.py:826
  71.4 2.7 %shard_map.138 = (bf16[48,32,128]{2,1,0:T(8,128)(2,1)}, f32[4,8,8,512]{3,2,1,0:T(8,128)}, f32[9,192,64]{2,1,0:T(8,128)}, f32[2,512,128]{2,1,0:T(8,128)}, f32[9,128,128]{2,1,0:T(8,128)}) custom-call(bf16[48,32,128]{2,1,0:T(8,128)(2,1)} %get-tuple-element.14.bev_in, f32[4,8,8,512]{3,2,1,0:T(8,128)} %get-tuple-element.15.feat_in, ...), custom_call_target="tpu_custom_call" | custom-call | tf_op jit(solution)/shard_map/pallas_call | solution.py:900
